TPU v7x, 32 devices: a whole 2x2x4 slice. The times are simulated.
32 devices in a mesh: slides: 2 (over y), row: 16 (over z, x, core), col: 1.
Axes of the slice: x: 2, y: 2, z: 4, core: 2. Of those that a mesh axis runs over, the one named last changes fastest.
Arguments:
- features: bfloat16 [128, 64, 2048], P(('slides', 'row'), 'col'), parts along dimension 0, may hold values from -6 to 6
- write_vecs: bfloat16 [128, 64, 128], P(('slides', 'row'), 'col'), parts along dimension 0, may hold values from -6 to 6
- read_vecs: bfloat16 [128, 64, 128], P(('slides', 'row'), 'col'), parts along dimension 0, may hold values from -0.119628906 to 0.119628906
- row_decay: bfloat16 [128, 64, 32], P(('slides', 'row'), 'col'), parts along dimension 0, may hold values from -1 to 0, as said below
- col_decay: bfloat16 [128, 64, 32], P(('slides', 'row'), 'col'), parts along dimension 0, may hold values from -1 to 0, as said below
- tile_mask: int32 [128, 1], P(('slides', 'row'), 'col'), parts along dimension 0, may hold values 0 or 1
- skip_gain: float32 [32], replicated, may hold values from 0.5 to 2
Outputs:
- mixed: bfloat16 [128, 64, 2048], P(('slides', 'row'), 'col'), parts along dimension 0
There are 2 independent parts, one for each index of `slides`. A program takes and returns all parts, laid end to end along the dimension named above; an argument that names none is the same for every part. Nothing has to cross between parts.
Inputs may be any that keep to these rules, and one draw needn't show every extreme that they name: `row_decay`: log decays of each patch and head along rows, never positive. `col_decay`: log decays of each patch and head along columns, never positive.
All inputs are finite; a program needn't handle non-finite values. No bound on the sum of `tile_mask` on one device may be relied on, other than what follows from the above.
Results may differ from a plain program's by a relative error of at most 0.005.
Values may be sent and summed in bfloat16 or wider, within the bound.
A program may use at most 128 MiB of HBM per device.

v0:
```python
import functools

import jax
import jax.numpy as jnp
from jax import lax
from jax.experimental import pallas as pl
from jax.experimental.pallas import tpu as pltpu
from jax.sharding import PartitionSpec as P


def entering_2(array, axis, combine, identity):
    devices, here = (lax.axis_size(axis), lax.axis_index(axis))
    everything = jax.tree.map(
        lambda part, kind: lax.all_gather(part.astype(kind), axis),
        array,
        (jnp.bfloat16, jnp.bfloat16),
    )
    start = jax.tree.map(
        lambda part, zero: jnp.broadcast_to(jnp.asarray(zero, part.dtype), part.shape),
        array,
        identity,
    )

    def step(k, before):
        reached = k < here
        new = combine(
            before, jax.tree.map(lambda part, own: part[k].astype(own.dtype), everything, array)
        )
        return jax.tree.map(lambda a, b: jnp.where(reached, a, b), new, before)

    return lax.fori_loop(0, devices, step, start)


def block_local(masked, write_vecs, read_vecs, decays):
    blocks, length, span_width = masked.shape
    head_count = decays.shape[-1]
    head_width = span_width // head_count
    slots = jnp.arange(length)
    upto = (slots[:, None] >= slots[None, :]).astype(decays.dtype)
    running = jnp.einsum("ts,ksh->kht", upto, decays, preferred_element_type=jnp.float32)
    scores = jnp.einsum("ktn,ksn->kts", read_vecs, write_vecs, preferred_element_type=jnp.float32)
    target_slots = jnp.arange(length)
    causal = target_slots[:, None] >= target_slots[None, :]
    spread = jnp.where(causal, running[:, :, :, None] - running[:, :, None, :], jnp.float32(0.0))
    weights = jnp.where(causal, scores[:, None] * jnp.exp(spread), jnp.float32(0.0)).astype(
        jnp.bfloat16
    )
    values = masked.reshape(blocks, length, head_count, head_width)
    inside = jnp.einsum("khts,kshp->kthp", weights, values, preferred_element_type=jnp.float32)
    closing = running[:, :, -1]
    scaled = (
        write_vecs.astype(jnp.float32)[:, None] * jnp.exp(closing[:, :, None] - running)[..., None]
    ).astype(jnp.bfloat16)
    block_state = jnp.einsum("khsn,kshp->khnp", scaled, values, preferred_element_type=jnp.float32)
    return (inside, block_state, jnp.exp(closing), running)


def enter_states(damping, block_state, initial):

    def advance(carry_state, element):
        factor, fresh_term = element
        return (factor[:, None, None] * carry_state + fresh_term, carry_state)

    return lax.scan(advance, initial, (damping, block_state))


def combine_out(inside, entering, read_blocks, running):
    carried = jnp.einsum(
        "ktn,khnp->kthp", read_blocks.astype(jnp.float32), entering, precision=lax.Precision.HIGHEST
    )
    total = inside + carried * jnp.swapaxes(jnp.exp(running), 1, 2)[..., None]
    return total.reshape(total.shape[0] * total.shape[1], total.shape[2] * total.shape[3])


def to_blocks(array, block_len):
    return array.reshape(
        array.shape[:-2] + (array.shape[-2] // block_len, block_len, array.shape[-1])
    )


def column_chains(masked, write_vecs, read_vecs, decays, block_len):

    def one_column(masked_c, write_c, read_c, decay_c):
        read_blocks = to_blocks(read_c, block_len)
        inside, block_state, damping, running = block_local(
            to_blocks(masked_c, block_len),
            to_blocks(write_c, block_len),
            read_blocks,
            to_blocks(decay_c, block_len),
        )
        if read_blocks.shape[0] == 1:
            return inside.reshape(masked_c.shape)
        zero_state = jnp.zeros(block_state.shape[1:], jnp.float32)
        closing_state, entering = enter_states(damping, block_state, zero_state)
        return combine_out(inside, entering, read_blocks, running)

    results = jax.vmap(one_column, in_axes=1, out_axes=1)(masked, write_vecs, read_vecs, decays)
    return results.astype(jnp.bfloat16)


def row_terms(masked, write_vecs, read_vecs, decays, block_len):
    read_blocks = to_blocks(read_vecs, block_len)
    local_terms = jax.vmap(block_local)(
        to_blocks(masked, block_len),
        to_blocks(write_vecs, block_len),
        read_blocks,
        to_blocks(decays, block_len),
    )
    return (local_terms, read_blocks)


def row_finish(local_terms, read_blocks, incoming):
    inside, block_state, damping, running = local_terms
    closing_state, entering = jax.vmap(enter_states)(damping, block_state, incoming)
    return jax.vmap(combine_out)(inside, entering, read_blocks, running)


def link(earlier, later):
    return (earlier[0] * later[0], later[0][..., None, None] * earlier[1] + later[1])


MESH = pl.DeviceIdType.MESH
CHUNKS = 4


def fused_kernel(
    shape,
    mask_ref,
    skip_ref,
    x_hbm,
    write_hbm,
    read_hbm,
    row_hbm,
    col_hbm,
    out_hbm,
    out_ref,
    x_ref,
    write_ref,
    read_ref,
    row_ref,
    col_ref,
    aux_out,
    aux_in,
    sent,
    got,
    col_sent,
    col_got,
    total,
    grow,
    fade,
    load_sems,
    x_sems,
    out_sems,
    aux_sems,
    there_sems,
    back_sems,
):
    devices, tile_rows, tile_cols, heads = shape
    per = tile_cols // devices
    block = tile_rows * per
    patches = tile_rows * tile_cols
    chunks, _, width = sent.shape
    head_width = chunks * width // heads
    state = write_ref.shape[-1]
    f32, bf16 = jnp.float32, jnp.bfloat16
    me = lax.axis_index("row")
    own = pl.ds(pl.multiple_of(me * block, block), block)

    def dot(a, b):
        return jnp.dot(a, b, preferred_element_type=f32)

    def peer(step):
        return lax.rem(me + 1 + step, devices)

    barrier = pltpu.get_barrier_semaphore()

    def greet(step, carry):
        pl.semaphore_signal(barrier, inc=1, device_id={"row": peer(step)}, device_id_type=MESH)
        return carry

    lax.fori_loop(0, devices - 1, greet, 0)
    loads = [
        pltpu.make_async_copy(source, target, load_sems.at[i])
        for i, (source, target) in enumerate(
            ((write_hbm, write_ref), (read_hbm, read_ref), (col_hbm, col_ref), (row_hbm, row_ref))
        )
    ]
    x_loads = [
        pltpu.make_async_copy(
            x_hbm.at[:, pl.ds(c * width, width)], x_ref.at[:, pl.ds(c * width, width)], x_sems.at[c]
        )
        for c in range(chunks)
    ]
    for load in loads[:3] + x_loads + loads[3:]:
        load.start()

    def scatter(source, target, sems):
        def send(step, carry):
            other = peer(step)
            pltpu.make_async_remote_copy(
                src_ref=source.at[pl.ds(pl.multiple_of(other * block, block), block)],
                dst_ref=target.at[own],
                send_sem=sems.at[0],
                recv_sem=sems.at[1],
                device_id={"row": other},
                device_id_type=MESH,
            ).start()
            return carry

        lax.fori_loop(0, devices - 1, send, 0)
        target[own, :] = source[own, :]

    def wait(buffer, sem):
        part = buffer.at[pl.ds(0, block * (devices - 1))]
        pltpu.make_async_copy(part, part, sem).wait()

    def shift(i, size):
        return lax.shift_right_logical(i, size.bit_length() - 1)

    down = lax.broadcasted_iota(jnp.int32, (patches, 1), 0)
    across = lax.broadcasted_iota(jnp.int32, (1, patches), 1)

    def home(i):
        row = shift(i, per) & (tile_rows - 1)
        return row * tile_cols + shift(i, block) * per + (i & (per - 1))

    def ones(where):
        return where.astype(f32).astype(bf16)

    from_home = home(down)
    order = ones(from_home == across)

    def turned(places, ref):
        lanes = lax.broadcasted_iota(jnp.int32, (1, tile_cols), 1)
        return sum(
            lax.dot_general(
                ones(places == lanes + r * tile_cols),
                ref[r],
                (((1,), (1,)), ((), ())),
                preferred_element_type=f32,
            )
            for r in range(tile_rows)
        ).astype(bf16)

    tile = [mask_ref[r].astype(f32) for r in range(tile_rows)]

    def keep(value):
        return jnp.concatenate(
            [value[r * tile_cols : (r + 1) * tile_cols] * tile[r] for r in range(tile_rows)]
        )

    aux_out[:, 2 * state :] = jnp.zeros((patches, aux_out.shape[1] - 2 * state), bf16)
    for load in loads[:3]:
        load.wait()
    aux_out[:, :state] = dot(order, write_ref[...]).astype(bf16)
    aux_out[:, state : 2 * state] = dot(order, read_ref[...]).astype(bf16)
    aux_out[:, 2 * state : 2 * state + heads] = turned(from_home, col_ref)
    pl.semaphore_wait(barrier, devices - 1)
    scatter(aux_out, aux_in, aux_sems)

    def masked(c):
        return keep(x_ref[:, c * width : (c + 1) * width].astype(f32)).astype(bf16)

    for c in range(chunks):
        x_loads[c].wait()
        sent[c] = dot(order, masked(c)).astype(bf16)
        scatter(sent.at[c], got.at[c], there_sems.at[c])

    def spread(c):
        head = lax.broadcasted_iota(jnp.int32, (heads, width), 0)
        lane = lax.broadcasted_iota(jnp.int32, (heads, width), 1)
        return (head == shift(lane + c * width, head_width)).astype(f32)

    def running(below, decays, c):
        return dot(below, dot(decays, spread(c).astype(bf16)).astype(bf16))

    def causal(reads, writes, allowed):
        scores = lax.dot_general(
            reads, writes, (((1,), (1,)), ((), ())), preferred_element_type=f32
        )
        return jnp.where(allowed, scores, 0.0).astype(bf16)

    restore = ones(down == home(across))
    in_row = (down >= across) & (shift(down, tile_cols) == shift(across, tile_cols))
    row_below = ones(in_row)
    loads[3].wait()
    row_decays = turned(down, row_ref)
    row_scores = causal(read_ref[...], write_ref[...], in_row)
    skip = jnp.broadcast_to(skip_ref[...], (8, heads))
    for c in range(chunks):
        cut = slice(c * width, (c + 1) * width)
        run = running(row_below, row_decays, c)
        faded = (masked(c).astype(f32) * jnp.exp(-run)).astype(bf16)
        gain = jnp.dot(
            skip, spread(c), precision=lax.Precision.HIGHEST, preferred_element_type=f32
        )[:1]
        total[:, cut] = jnp.exp(run) * dot(row_scores, faded) + gain * x_ref[:, cut].astype(f32)

    in_col = (down >= across) & ((down & (per - 1)) == (across & (per - 1)))
    col_below = ones(in_col)
    wait(aux_in, aux_sems.at[1])
    col_scores = causal(aux_in[:, state : 2 * state], aux_in[:, :state], in_col)
    for c in range(chunks):
        run = running(col_below, aux_in[:, 2 * state : 2 * state + heads], c)
        grow[c] = jnp.exp(run)
        fade[c] = jnp.exp(-run)

    for c in range(chunks):
        wait(got.at[c], there_sems.at[c, 1])
        faded = (got[c].astype(f32) * fade[c]).astype(bf16)
        col_sent[c] = (grow[c] * dot(col_scores, faded)).astype(bf16)
        scatter(col_sent.at[c], col_got.at[c], back_sems.at[c])

    stores = []
    for c in range(chunks):
        cut = slice(c * width, (c + 1) * width)
        wait(col_got.at[c], back_sems.at[c, 1])
        out_ref[:, cut] = keep(total[:, cut] + dot(restore, col_got[c])).astype(bf16)
        part = pl.ds(c * width, width)
        stores.append(
            pltpu.make_async_copy(out_ref.at[:, part], out_hbm.at[:, part], out_sems.at[c])
        )
        stores[c].start()

    wait(aux_out, aux_sems.at[0])
    for c in range(chunks):
        wait(sent.at[c], there_sems.at[c, 0])
        wait(col_sent.at[c], back_sems.at[c, 0])
        stores[c].wait()


def fused(features, write_vecs, read_vecs, row_decay, col_decay, tile_mask, skip_gain):
    tile_rows, tile_cols, span_width = features.shape
    heads, state = row_decay.shape[-1], write_vecs.shape[-1]
    patches = tile_rows * tile_cols
    devices = lax.axis_size("row")
    width = span_width // CHUNKS

    def flat(array):
        return array.reshape(patches, array.shape[-1])

    vmem = pl.BlockSpec(memory_space=pltpu.VMEM)
    piece = (CHUNKS, patches, width)
    aux = pltpu.VMEM((patches, 2 * state + 128), jnp.bfloat16)
    result = pl.pallas_call(
        functools.partial(fused_kernel, (devices, tile_rows, tile_cols, heads)),
        out_shape=jax.ShapeDtypeStruct((patches, span_width), jnp.bfloat16),
        in_specs=[pl.BlockSpec(memory_space=pltpu.SMEM), vmem]
        + [pl.BlockSpec(memory_space=pl.ANY)] * 5,
        out_specs=pl.BlockSpec(memory_space=pl.ANY),
        scratch_shapes=[
            pltpu.VMEM((patches, span_width), jnp.bfloat16),
            pltpu.VMEM((patches, span_width), jnp.bfloat16),
            pltpu.VMEM((patches, state), jnp.bfloat16),
            pltpu.VMEM((patches, state), jnp.bfloat16),
            pltpu.VMEM((tile_rows, heads, tile_cols), jnp.bfloat16),
            pltpu.VMEM((tile_rows, heads, tile_cols), jnp.bfloat16),
            aux,
            aux,
            pltpu.VMEM(piece, jnp.bfloat16),
            pltpu.VMEM(piece, jnp.bfloat16),
            pltpu.VMEM(piece, jnp.bfloat16),
            pltpu.VMEM(piece, jnp.bfloat16),
            pltpu.VMEM((patches, span_width), jnp.float32),
            pltpu.VMEM(piece, jnp.float32),
            pltpu.VMEM(piece, jnp.float32),
            pltpu.SemaphoreType.DMA((4,)),
            pltpu.SemaphoreType.DMA((CHUNKS,)),
            pltpu.SemaphoreType.DMA((CHUNKS,)),
            pltpu.SemaphoreType.DMA((2,)),
            pltpu.SemaphoreType.DMA((CHUNKS, 2)),
            pltpu.SemaphoreType.DMA((CHUNKS, 2)),
        ],
        compiler_params=pltpu.CompilerParams(
            collective_id=0, has_side_effects=True, vmem_limit_bytes=60 * 2**20
        ),
    )(
        tile_mask.reshape(-1),
        skip_gain.reshape(1, heads),
        flat(features),
        flat(write_vecs),
        flat(read_vecs),
        jnp.swapaxes(row_decay, 1, 2),
        jnp.swapaxes(col_decay, 1, 2),
    )
    return result.reshape(features.shape)


def fits_fused(features, row_decay, tile_mask):
    tile_rows, tile_cols, span_width = features.shape
    devices = lax.axis_size("row")
    return (
        lax.axis_size("col") == 1
        and tile_mask.shape[1] == 1
        and tile_rows * devices == tile_cols
        and tile_cols <= 64
        and (tile_rows * (tile_cols // devices)) % 16 == 0
        and span_width % (CHUNKS * 128) == 0
        and row_decay.shape[-1] <= 128
        and all(
            size.bit_count() == 1
            for size in (tile_rows, tile_cols, devices, span_width // row_decay.shape[-1])
        )
    )


def per_device(features, write_vecs, read_vecs, row_decay, col_decay, tile_mask, skip_gain):
    tile_rows, tile_cols, span_width = features.shape
    if fits_fused(features, row_decay, tile_mask):
        return fused(features, write_vecs, read_vecs, row_decay, col_decay, tile_mask, skip_gain)
    head_count = row_decay.shape[-1]
    block_len = tile_cols // tile_mask.shape[1]
    patch_mask = jnp.repeat(tile_mask, block_len, axis=1)
    masked = jnp.where(patch_mask[..., None] > 0, features, jnp.zeros((), features.dtype))
    moved = (
        lax.all_to_all(masked, "row", split_axis=1, concat_axis=0, tiled=True),
        lax.all_to_all(write_vecs, "row", split_axis=1, concat_axis=0, tiled=True),
        lax.all_to_all(read_vecs, "row", split_axis=1, concat_axis=0, tiled=True),
        lax.all_to_all(col_decay, "row", split_axis=1, concat_axis=0, tiled=True),
    )
    result = column_chains(moved[0], moved[1], moved[2], moved[3], block_len)
    col_out = lax.all_to_all(result, "row", split_axis=0, concat_axis=1, tiled=True)
    local_terms, read_blocks = row_terms(masked, write_vecs, read_vecs, row_decay, block_len)
    if lax.axis_size("col") == 1 and tile_mask.shape[1] == 1:
        y_row = local_terms[0].reshape(features.shape)
    else:
        zero_states = jnp.zeros((tile_rows,) + local_terms[1].shape[2:], jnp.float32)
        closing_states, unused_states = jax.vmap(enter_states)(
            local_terms[2], local_terms[1], zero_states
        )
        device_decay = jnp.prod(local_terms[2], axis=1)
        identity = (jnp.ones_like(device_decay), jnp.zeros_like(closing_states))
        decay_before, state_before = entering_2((device_decay, closing_states), "col", link, identity)
        y_row = row_finish(local_terms, read_blocks, state_before)
    skip_vector = jnp.repeat(skip_gain, span_width // head_count)
    total = y_row + col_out.astype(jnp.float32) + skip_vector * features.astype(jnp.float32)
    return (patch_mask[..., None].astype(jnp.float32) * total).astype(jnp.bfloat16)


def solution(mesh):
    return jax.shard_map(
        per_device,
        mesh=mesh,
        in_specs=(
            P(("slides", "row"), "col", None),
            P(("slides", "row"), "col", None),
            P(("slides", "row"), "col", None),
            P(("slides", "row"), "col", None),
            P(("slides", "row"), "col", None),
            P(("slides", "row"), "col"),
            P(),
        ),
        out_specs=P(("slides", "row"), "col", None),
        check_vma=False,
    )
```

profile of v0, /device:TPU:31, one launch (start us, length us, event | category | flops | bytes accessed | tf_op | source)
XLA Modules:
  0.0 58.4 jit_solution(446492866003962291)
XLA Ops:
  0.0 56.1 %shard_map.73 = bf16[256,2048]{1,0:T(8,128)(2,1)} custom-call(s32[4]{0:T(128)} %bitcast.14, f32[1,32]{1,0:T(1,128)} %bitcast.15, bf16[256,2048]{1,0:T(8,128)(2,1)} %bitcast.9, bf16[256,128]{1,0:T(8,128)(2,1)} %bitcast.10, bf16[256,128]{1,0:T(8,128)(2,1)} %bitcast.11, bf16[4,32,64]{2,1,0:T(8,128)(2,1)} %bitcast.12, bf16[4,32,64]{2,1,0:T(8,128)(2,1)} %bitcast.13), custom_call_target="tpu_custom_call" | custom-call | tf_op jit(solution)/shard_map/pallas_call | solution.py:345
  56.1 2.3 %copy.9 = bf16[4,64,2048]{2,1,0:T(8,128)(2,1)} copy(bf16[4,64,2048]{2,1,0:T(8,128)(2,1)} %bitcast.8) | data formatting | bytes 2097152
where the time goes:
time: 59.3 us; the launch traced here: 58.4 us
  Pallas kernels  56.1 us (95%)
  local copies, waits for them, and re-layouts  2.3 us (4%)
    pallas_call x1, Pallas kernels, fused(): pl.pallas_call(functools.partial(fused_kernel, (devices, tile_rows, tile_...  56.1 us
    unnamed x1, local copies, waits for them, and re-layouts  2.3 us

commit v1 on v0

--- a/solution.py
+++ b/solution.py
@@ -132,7 +132,6 @@
     read_hbm,
     row_hbm,
     col_hbm,
-    out_hbm,
     out_ref,
     x_ref,
     write_ref,
@@ -150,7 +149,6 @@
     fade,
     load_sems,
     x_sems,
-    out_sems,
     aux_sems,
     there_sems,
     back_sems,
@@ -311,22 +309,15 @@
         col_sent[c] = (grow[c] * dot(col_scores, faded)).astype(bf16)
         scatter(col_sent.at[c], col_got.at[c], back_sems.at[c])
 
-    stores = []
     for c in range(chunks):
         cut = slice(c * width, (c + 1) * width)
         wait(col_got.at[c], back_sems.at[c, 1])
         out_ref[:, cut] = keep(total[:, cut] + dot(restore, col_got[c])).astype(bf16)
-        part = pl.ds(c * width, width)
-        stores.append(
-            pltpu.make_async_copy(out_ref.at[:, part], out_hbm.at[:, part], out_sems.at[c])
-        )
-        stores[c].start()
 
     wait(aux_out, aux_sems.at[0])
     for c in range(chunks):
         wait(sent.at[c], there_sems.at[c, 0])
         wait(col_sent.at[c], back_sems.at[c, 0])
-        stores[c].wait()
 
 
 def fused(features, write_vecs, read_vecs, row_decay, col_decay, tile_mask, skip_gain):
@@ -344,12 +335,11 @@
     aux = pltpu.VMEM((patches, 2 * state + 128), jnp.bfloat16)
     result = pl.pallas_call(
         functools.partial(fused_kernel, (devices, tile_rows, tile_cols, heads)),
-        out_shape=jax.ShapeDtypeStruct((patches, span_width), jnp.bfloat16),
+        out_shape=pltpu.VMEM((patches, span_width), jnp.bfloat16),
         in_specs=[pl.BlockSpec(memory_space=pltpu.SMEM), vmem]
         + [pl.BlockSpec(memory_space=pl.ANY)] * 5,
-        out_specs=pl.BlockSpec(memory_space=pl.ANY),
+        out_specs=vmem,
         scratch_shapes=[
-            pltpu.VMEM((patches, span_width), jnp.bfloat16),
             pltpu.VMEM((patches, span_width), jnp.bfloat16),
             pltpu.VMEM((patches, state), jnp.bfloat16),
             pltpu.VMEM((patches, state), jnp.bfloat16),
@@ -366,7 +356,6 @@
             pltpu.VMEM(piece, jnp.float32),
             pltpu.SemaphoreType.DMA((4,)),
             pltpu.SemaphoreType.DMA((CHUNKS,)),
-            pltpu.SemaphoreType.DMA((CHUNKS,)),
             pltpu.SemaphoreType.DMA((2,)),
             pltpu.SemaphoreType.DMA((CHUNKS, 2)),
             pltpu.SemaphoreType.DMA((CHUNKS, 2)),

time: 59.3 us -> 57.2 us (0.965)
  local copies, waits for them, and re-layouts: 2.3 us -> 0.97 us
  Pallas kernels: 56.1 us -> 55.3 us
    unnamed x1, local copies, waits for them, and re-layouts: 2.3 us -> 0.97 us
    pallas_call x1, Pallas kernels: 56.1 us -> 55.3 us  [fused(): pl.pallas_call(functools.partial(fused_kernel, (devices, tile_rows, tile_...]
where the time goes in v1:
time: 57.2 us; the launch traced here: 56.3 us
  Pallas kernels  55.3 us (97%)
  local copies, waits for them, and re-layouts  0.97 us (2%)
    pallas_call x1, Pallas kernels, fused(): pl.pallas_call(functools.partial(fused_kernel, (devices, tile_rows, tile_...  55.3 us

profile of v1, /device:TPU:31, one launch (start us, length us, event | category | flops | bytes accessed | tf_op | source)
XLA Modules:
  0.0 56.3 jit_solution(7826207961363891066)
XLA Ops:
  0.0 55.3 %shard_map.73 = bf16[256,2048]{1,0:T(8,128)(2,1)S(1)} custom-call(s32[4]{0:T(128)} %bitcast.14, f32[1,32]{1,0:T(1,128)} %bitcast.15, bf16[256,2048]{1,0:T(8,128)(2,1)} %bitcast.9, bf16[256,128]{1,0:T(8,128)(2,1)} %bitcast.10, bf16[256,128]{1,0:T(8,128)(2,1)} %bitcast.11, bf16[4,32,64]{2,1,0:T(8,128)(2,1)} %bitcast.12, bf16[4,32,64]{2,1,0:T(8,128)(2,1)} %bitcast.13), custom_call_target="tpu_custom_call" | custom-call | tf_op jit(solution)/shard_map/pallas_call | solution.py:336
  55.3 1.0 %copy.9 = bf16[4,64,2048]{2,1,0:T(8,128)(2,1)} copy(bf16[4,64,2048]{2,1,0:T(8,128)(2,1)S(1)} %bitcast.8) | data formatting | bytes 2097152

commit v2 on v1

--- a/solution.py
+++ b/solution.py
@@ -125,14 +125,16 @@
 
 def fused_kernel(
     shape,
-    mask_ref,
-    skip_ref,
+    mask_hbm,
+    skip_hbm,
     x_hbm,
     write_hbm,
     read_hbm,
     row_hbm,
     col_hbm,
     out_ref,
+    mask_ref,
+    skip_ref,
     x_ref,
     write_ref,
     read_ref,
@@ -180,7 +182,14 @@
     loads = [
         pltpu.make_async_copy(source, target, load_sems.at[i])
         for i, (source, target) in enumerate(
-            ((write_hbm, write_ref), (read_hbm, read_ref), (col_hbm, col_ref), (row_hbm, row_ref))
+            (
+                (mask_hbm, mask_ref),
+                (write_hbm, write_ref),
+                (read_hbm, read_ref),
+                (col_hbm, col_ref),
+                (row_hbm, row_ref),
+                (skip_hbm, skip_ref),
+            )
         )
     ]
     x_loads = [
@@ -189,7 +198,7 @@
         )
         for c in range(chunks)
     ]
-    for load in loads[:3] + x_loads + loads[3:]:
+    for load in loads[:4] + x_loads + loads[4:]:
         load.start()
 
     def scatter(source, target, sems):
@@ -240,6 +249,9 @@
             for r in range(tile_rows)
         ).astype(bf16)
 
+    aux_out[:, 2 * state :] = jnp.zeros((patches, aux_out.shape[1] - 2 * state), bf16)
+    for load in loads[:4]:
+        load.wait()
     tile = [mask_ref[r].astype(f32) for r in range(tile_rows)]
 
     def keep(value):
@@ -247,21 +259,15 @@
             [value[r * tile_cols : (r + 1) * tile_cols] * tile[r] for r in range(tile_rows)]
         )
 
-    aux_out[:, 2 * state :] = jnp.zeros((patches, aux_out.shape[1] - 2 * state), bf16)
-    for load in loads[:3]:
-        load.wait()
-    aux_out[:, :state] = dot(order, write_ref[...]).astype(bf16)
+    aux_out[:, :state] = dot(order, keep(write_ref[...].astype(f32)).astype(bf16)).astype(bf16)
     aux_out[:, state : 2 * state] = dot(order, read_ref[...]).astype(bf16)
     aux_out[:, 2 * state : 2 * state + heads] = turned(from_home, col_ref)
     pl.semaphore_wait(barrier, devices - 1)
     scatter(aux_out, aux_in, aux_sems)
 
-    def masked(c):
-        return keep(x_ref[:, c * width : (c + 1) * width].astype(f32)).astype(bf16)
-
     for c in range(chunks):
         x_loads[c].wait()
-        sent[c] = dot(order, masked(c)).astype(bf16)
+        sent[c] = dot(order, x_ref[:, c * width : (c + 1) * width]).astype(bf16)
         scatter(sent.at[c], got.at[c], there_sems.at[c])
 
     def spread(c):
@@ -281,14 +287,15 @@
     restore = ones(down == home(across))
     in_row = (down >= across) & (shift(down, tile_cols) == shift(across, tile_cols))
     row_below = ones(in_row)
-    loads[3].wait()
+    for load in loads[4:]:
+        load.wait()
     row_decays = turned(down, row_ref)
     row_scores = causal(read_ref[...], write_ref[...], in_row)
     skip = jnp.broadcast_to(skip_ref[...], (8, heads))
     for c in range(chunks):
         cut = slice(c * width, (c + 1) * width)
         run = running(row_below, row_decays, c)
-        faded = (masked(c).astype(f32) * jnp.exp(-run)).astype(bf16)
+        faded = (x_ref[:, cut].astype(f32) * jnp.exp(-run)).astype(bf16)
         gain = jnp.dot(
             skip, spread(c), precision=lax.Precision.HIGHEST, preferred_element_type=f32
         )[:1]
@@ -336,10 +343,11 @@
     result = pl.pallas_call(
         functools.partial(fused_kernel, (devices, tile_rows, tile_cols, heads)),
         out_shape=pltpu.VMEM((patches, span_width), jnp.bfloat16),
-        in_specs=[pl.BlockSpec(memory_space=pltpu.SMEM), vmem]
-        + [pl.BlockSpec(memory_space=pl.ANY)] * 5,
+        in_specs=[pl.BlockSpec(memory_space=pl.ANY)] * 7,
         out_specs=vmem,
         scratch_shapes=[
+            pltpu.SMEM((tile_rows,), jnp.int32),
+            pltpu.VMEM((1, heads), jnp.float32),
             pltpu.VMEM((patches, span_width), jnp.bfloat16),
             pltpu.VMEM((patches, state), jnp.bfloat16),
             pltpu.VMEM((patches, state), jnp.bfloat16),
@@ -354,7 +362,7 @@
             pltpu.VMEM((patches, span_width), jnp.float32),
             pltpu.VMEM(piece, jnp.float32),
             pltpu.VMEM(piece, jnp.float32),
-            pltpu.SemaphoreType.DMA((4,)),
+            pltpu.SemaphoreType.DMA((6,)),
             pltpu.SemaphoreType.DMA((CHUNKS,)),
             pltpu.SemaphoreType.DMA((2,)),
             pltpu.SemaphoreType.DMA((CHUNKS, 2)),

time: 57.2 us -> 56.4 us (0.986)
  Pallas kernels: 55.3 us -> 54.6 us
    pallas_call x1, Pallas kernels: 55.3 us -> 54.6 us  [fused(): pl.pallas_call(functools.partial(fused_kernel, (devices, tile_rows, tile_...]
where the time goes in v2:
time: 56.4 us; the launch traced here: 55.6 us
  Pallas kernels  54.6 us (97%)
  local copies, waits for them, and re-layouts  0.97 us (2%)
    pallas_call x1, Pallas kernels, fused(): pl.pallas_call(functools.partial(fused_kernel, (devices, tile_rows, tile_...  54.6 us

profile of v2, /device:TPU:31, one launch (start us, length us, event | category | flops | bytes accessed | tf_op | source)
XLA Modules:
  0.0 55.6 jit_solution(2816242542125233029)
XLA Ops:
  0.0 54.6 %shard_map.73 = bf16[256,2048]{1,0:T(8,128)(2,1)S(1)} custom-call(s32[4]{0:T(128)} %bitcast.14, f32[1,32]{1,0:T(1,128)} %bitcast.15, bf16[256,2048]{1,0:T(8,128)(2,1)} %bitcast.9, bf16[256,128]{1,0:T(8,128)(2,1)} %bitcast.10, bf16[256,128]{1,0:T(8,128)(2,1)} %bitcast.11, bf16[4,32,64]{2,1,0:T(8,128)(2,1)} %bitcast.12, bf16[4,32,64]{2,1,0:T(8,128)(2,1)} %bitcast.13), custom_call_target="tpu_custom_call" | custom-call | tf_op jit(solution)/shard_map/pallas_call | solution.py:343
  54.6 1.0 %copy.9 = bf16[4,64,2048]{2,1,0:T(8,128)(2,1)} copy(bf16[4,64,2048]{2,1,0:T(8,128)(2,1)S(1)} %bitcast.8) | data formatting | bytes 2097152

commit v3 on v2

--- a/solution.py
+++ b/solution.py
@@ -154,6 +154,7 @@
     aux_sems,
     there_sems,
     back_sems,
+    late_sem,
 ):
     devices, tile_rows, tile_cols, heads = shape
     per = tile_cols // devices
@@ -169,16 +170,40 @@
     def dot(a, b):
         return jnp.dot(a, b, preferred_element_type=f32)
 
+    quarter = devices // 4
+    first = devices - quarter
+    last = me >= first
+    soon = jnp.where(last, devices - 1, first - 1)
+
     def peer(step):
         return lax.rem(me + 1 + step, devices)
 
+    def soon_peer(step):
+        return lax.rem(me + 1 + step, soon + 1)
+
+    def late_peer(step):
+        return first + lax.rem(me + step, quarter)
+
     barrier = pltpu.get_barrier_semaphore()
 
-    def greet(step, carry):
-        pl.semaphore_signal(barrier, inc=1, device_id={"row": peer(step)}, device_id_type=MESH)
-        return carry
-
-    lax.fori_loop(0, devices - 1, greet, 0)
+    def each(steps, act):
+        def body(step, carry):
+            act(step)
+            return carry
+
+        lax.fori_loop(0, steps, body, 0)
+
+    def greet(other, semaphore=barrier):
+        pl.semaphore_signal(semaphore, inc=1, device_id={"row": other}, device_id_type=MESH)
+
+    @pl.when(last)
+    def _():
+        each(quarter - 1, lambda step: greet(first + lax.rem(me + 1 + step, quarter)))
+
+    @pl.when(jnp.logical_not(last))
+    def _():
+        each(devices - 1, lambda step: greet(peer(step)))
+
     loads = [
         pltpu.make_async_copy(source, target, load_sems.at[i])
         for i, (source, target) in enumerate(
@@ -201,21 +226,26 @@
     for load in loads[:4] + x_loads + loads[4:]:
         load.start()
 
+    def send(source, target, sems, other):
+        pltpu.make_async_remote_copy(
+            src_ref=source.at[pl.ds(pl.multiple_of(other * block, block), block)],
+            dst_ref=target.at[own],
+            send_sem=sems.at[0],
+            recv_sem=sems.at[1],
+            device_id={"row": other},
+            device_id_type=MESH,
+        ).start()
+
     def scatter(source, target, sems):
-        def send(step, carry):
-            other = peer(step)
-            pltpu.make_async_remote_copy(
-                src_ref=source.at[pl.ds(pl.multiple_of(other * block, block), block)],
-                dst_ref=target.at[own],
-                send_sem=sems.at[0],
-                recv_sem=sems.at[1],
-                device_id={"row": other},
-                device_id_type=MESH,
-            ).start()
-            return carry
-
-        lax.fori_loop(0, devices - 1, send, 0)
+        each(devices - 1, lambda step: send(source, target, sems, peer(step)))
         target[own, :] = source[own, :]
+
+    def scatter_soon(source, target, sems):
+        each(soon, lambda step: send(source, target, sems, soon_peer(step)))
+        target[own, :] = source[own, :]
+
+    def scatter_late(source, target, sems):
+        each(quarter, lambda step: send(source, target, sems, late_peer(step)))
 
     def wait(buffer, sem):
         part = buffer.at[pl.ds(0, block * (devices - 1))]
@@ -262,13 +292,31 @@
     aux_out[:, :state] = dot(order, keep(write_ref[...].astype(f32)).astype(bf16)).astype(bf16)
     aux_out[:, state : 2 * state] = dot(order, read_ref[...]).astype(bf16)
     aux_out[:, 2 * state : 2 * state + heads] = turned(from_home, col_ref)
-    pl.semaphore_wait(barrier, devices - 1)
-    scatter(aux_out, aux_in, aux_sems)
+
+    @pl.when(last)
+    def _():
+        pl.semaphore_wait(barrier, devices - 1)
+        each(first, lambda step: greet(lax.rem(me + step, first), late_sem))
+
+    @pl.when(jnp.logical_not(last))
+    def _():
+        pl.semaphore_wait(barrier, first - 1)
+
+    scatter_soon(aux_out, aux_in, aux_sems)
 
     for c in range(chunks):
         x_loads[c].wait()
         sent[c] = dot(order, x_ref[:, c * width : (c + 1) * width]).astype(bf16)
-        scatter(sent.at[c], got.at[c], there_sems.at[c])
+        if c:
+            scatter(sent.at[c], got.at[c], there_sems.at[c])
+            continue
+        scatter_soon(sent.at[c], got.at[c], there_sems.at[c])
+
+        @pl.when(jnp.logical_not(last))
+        def _():
+            pl.semaphore_wait(late_sem, quarter)
+            scatter_late(aux_out, aux_in, aux_sems)
+            scatter_late(sent.at[c], got.at[c], there_sems.at[c])
 
     def spread(c):
         head = lax.broadcasted_iota(jnp.int32, (heads, width), 0)
@@ -367,6 +415,7 @@
             pltpu.SemaphoreType.DMA((2,)),
             pltpu.SemaphoreType.DMA((CHUNKS, 2)),
             pltpu.SemaphoreType.DMA((CHUNKS, 2)),
+            pltpu.SemaphoreType.REGULAR,
         ],
         compiler_params=pltpu.CompilerParams(
             collective_id=0, has_side_effects=True, vmem_limit_bytes=60 * 2**20
@@ -390,6 +439,7 @@
         lax.axis_size("col") == 1
         and tile_mask.shape[1] == 1
         and tile_rows * devices == tile_cols
+        and devices % 4 == 0
         and tile_cols <= 64
         and (tile_rows * (tile_cols // devices)) % 16 == 0
         and span_width % (CHUNKS * 128) == 0

time: 56.4 us -> 56.2 us (level)
  the two profiles are of different devices: /device:TPU:31 before, /device:TPU:0 now
where the time goes in v3:
time: 56.2 us; the launch traced here: 56.1 us
  Pallas kernels  55.1 us (98%)
  local copies, waits for them, and re-layouts  0.97 us (2%)
    pallas_call x1, Pallas kernels, fused(): pl.pallas_call(functools.partial(fused_kernel, (devices, tile_rows, tile_...  55.1 us

profile of v3, /device:TPU:0, one launch (start us, length us, event | category | flops | bytes accessed | tf_op | source)
XLA Modules:
  0.0 56.1 jit_solution(28151516882293844)
XLA Ops:
  0.0 55.1 %shard_map.73 = bf16[256,2048]{1,0:T(8,128)(2,1)S(1)} custom-call(s32[4]{0:T(128)} %bitcast.14, f32[1,32]{1,0:T(1,128)} %bitcast.15, bf16[256,2048]{1,0:T(8,128)(2,1)} %bitcast.9, bf16[256,128]{1,0:T(8,128)(2,1)} %bitcast.10, bf16[256,128]{1,0:T(8,128)(2,1)} %bitcast.11, bf16[4,32,64]{2,1,0:T(8,128)(2,1)} %bitcast.12, bf16[4,32,64]{2,1,0:T(8,128)(2,1)} %bitcast.13), custom_call_target="tpu_custom_call" | custom-call | tf_op jit(solution)/shard_map/pallas_call | solution.py:391
  55.1 1.0 %copy.9 = bf16[4,64,2048]{2,1,0:T(8,128)(2,1)} copy(bf16[4,64,2048]{2,1,0:T(8,128)(2,1)S(1)} %bitcast.8) | data formatting | bytes 2097152

commit v4 on v3

--- a/solution.py
+++ b/solution.py
@@ -236,20 +236,37 @@
             device_id_type=MESH,
         ).start()
 
-    def scatter(source, target, sems):
-        each(devices - 1, lambda step: send(source, target, sems, peer(step)))
-        target[own, :] = source[own, :]
+    tail = me == devices - 1
+    head = me == 0
 
     def scatter_soon(source, target, sems):
         each(soon, lambda step: send(source, target, sems, soon_peer(step)))
-        target[own, :] = source[own, :]
 
     def scatter_late(source, target, sems):
         each(quarter, lambda step: send(source, target, sems, late_peer(step)))
 
-    def wait(buffer, sem):
-        part = buffer.at[pl.ds(0, block * (devices - 1))]
+    def give_back(source, target, sems):
+        def act(step):
+            other = peer(step)
+
+            @pl.when(other != 0)
+            def _():
+                send(source, target, sems, other)
+
+        each(devices - 1, act)
+
+    def wait(buffer, sem, count=devices - 1):
+        part = buffer.at[pl.ds(0, block * count)]
         pltpu.make_async_copy(part, part, sem).wait()
+
+    def wait_either(buffer, sem, all_of_them):
+        @pl.when(all_of_them)
+        def _():
+            wait(buffer, sem)
+
+        @pl.when(jnp.logical_not(all_of_them))
+        def _():
+            wait(buffer, sem, devices - 2)
 
     def shift(i, size):
         return lax.shift_right_logical(i, size.bit_length() - 1)
@@ -303,20 +320,28 @@
         pl.semaphore_wait(barrier, first - 1)
 
     scatter_soon(aux_out, aux_in, aux_sems)
+    aux_in[own, :] = aux_out[own, :]
 
     for c in range(chunks):
         x_loads[c].wait()
         sent[c] = dot(order, x_ref[:, c * width : (c + 1) * width]).astype(bf16)
-        if c:
-            scatter(sent.at[c], got.at[c], there_sems.at[c])
-            continue
-        scatter_soon(sent.at[c], got.at[c], there_sems.at[c])
-
-        @pl.when(jnp.logical_not(last))
+        got[c, block * (devices - 1) :, :] = jnp.zeros((block, width), bf16)
+        got[c, own, :] = sent[c, own, :]
+
+        @pl.when(jnp.logical_not(tail))
         def _():
-            pl.semaphore_wait(late_sem, quarter)
-            scatter_late(aux_out, aux_in, aux_sems)
-            scatter_late(sent.at[c], got.at[c], there_sems.at[c])
+            if c:
+                each(devices - 1, lambda step: send(sent.at[c], got.at[c], there_sems.at[c], peer(step)))
+            else:
+                scatter_soon(sent.at[c], got.at[c], there_sems.at[c])
+
+        if not c:
+
+            @pl.when(jnp.logical_not(last))
+            def _():
+                pl.semaphore_wait(late_sem, quarter)
+                scatter_late(aux_out, aux_in, aux_sems)
+                scatter_late(sent.at[c], got.at[c], there_sems.at[c])
 
     def spread(c):
         head = lax.broadcasted_iota(jnp.int32, (heads, width), 0)
@@ -326,10 +351,12 @@
     def running(below, decays, c):
         return dot(below, dot(decays, spread(c).astype(bf16)).astype(bf16))
 
-    def causal(reads, writes, allowed):
-        scores = lax.dot_general(
+    def products(reads, writes):
+        return lax.dot_general(
             reads, writes, (((1,), (1,)), ((), ())), preferred_element_type=f32
         )
+
+    def causal(scores, allowed):
         return jnp.where(allowed, scores, 0.0).astype(bf16)
 
     restore = ones(down == home(across))
@@ -338,7 +365,14 @@
     for load in loads[4:]:
         load.wait()
     row_decays = turned(down, row_ref)
-    row_scores = causal(read_ref[...], write_ref[...], in_row)
+    own_scores = products(read_ref[...], write_ref[...])
+    row_scores = causal(own_scores, in_row)
+    in_home = (down >= across) & ((down & (tile_cols - 1)) == (across & (tile_cols - 1)))
+    home_below = ones(in_home)
+    home_decays = turned(down, col_ref)
+    origin = shift(across, tile_cols)
+    present = sum(jnp.where(origin == r, tile[r], 0.0) for r in range(tile_rows))
+    home_scores = causal(own_scores * present, in_home)
     skip = jnp.broadcast_to(skip_ref[...], (8, heads))
     for c in range(chunks):
         cut = slice(c * width, (c + 1) * width)
@@ -349,30 +383,47 @@
         )[:1]
         total[:, cut] = jnp.exp(run) * dot(row_scores, faded) + gain * x_ref[:, cut].astype(f32)
 
-    in_col = (down >= across) & ((down & (per - 1)) == (across & (per - 1)))
-    col_below = ones(in_col)
+    same_col = (down & (per - 1)) == (across & (per - 1))
+    col_below = ones((down >= across) & same_col)
     wait(aux_in, aux_sems.at[1])
-    col_scores = causal(aux_in[:, state : 2 * state], aux_in[:, :state], in_col)
+    earlier = (shift(down, block) > shift(across, block)) & same_col
+    col_scores = causal(products(aux_in[:, state : 2 * state], aux_in[:, :state]), earlier)
     for c in range(chunks):
         run = running(col_below, aux_in[:, 2 * state : 2 * state + heads], c)
         grow[c] = jnp.exp(run)
         fade[c] = jnp.exp(-run)
 
     for c in range(chunks):
-        wait(got.at[c], there_sems.at[c, 1])
+        wait_either(got.at[c], there_sems.at[c, 1], tail)
         faded = (got[c].astype(f32) * fade[c]).astype(bf16)
         col_sent[c] = (grow[c] * dot(col_scores, faded)).astype(bf16)
-        scatter(col_sent.at[c], col_got.at[c], back_sems.at[c])
+        give_back(col_sent.at[c], col_got.at[c], back_sems.at[c])
+        col_got[c, own, :] = col_sent[c, own, :]
+        cut = slice(c * width, (c + 1) * width)
+        run = running(home_below, home_decays, c)
+        faded = (x_ref[:, cut].astype(f32) * jnp.exp(-run)).astype(bf16)
+        total[:, cut] += jnp.exp(run) * dot(home_scores, faded)
 
     for c in range(chunks):
         cut = slice(c * width, (c + 1) * width)
-        wait(col_got.at[c], back_sems.at[c, 1])
+
+        @pl.when(head)
+        def _():
+            col_got[c] = jnp.zeros((patches, width), bf16)
+
+        @pl.when(jnp.logical_not(head))
+        def _():
+            wait(col_got.at[c], back_sems.at[c, 1])
+
         out_ref[:, cut] = keep(total[:, cut] + dot(restore, col_got[c])).astype(bf16)
 
     wait(aux_out, aux_sems.at[0])
     for c in range(chunks):
-        wait(sent.at[c], there_sems.at[c, 0])
-        wait(col_sent.at[c], back_sems.at[c, 0])
+        wait_either(col_sent.at[c], back_sems.at[c, 0], head)
+
+        @pl.when(jnp.logical_not(tail))
+        def _():
+            wait(sent.at[c], there_sems.at[c, 0])
 
 
 def fused(features, write_vecs, read_vecs, row_decay, col_decay, tile_mask, skip_gain):

time: 56.2 us -> 54.7 us (0.973)
  the two profiles are of different devices: /device:TPU:0 before, /device:TPU:31 now
where the time goes in v4:
time: 54.7 us; the launch traced here: 54.6 us
  Pallas kernels  53.6 us (98%)
  local copies, waits for them, and re-layouts  0.97 us (2%)
    pallas_call x1, Pallas kernels, fused(): pl.pallas_call(functools.partial(fused_kernel, (devices, tile_rows, tile_...  53.6 us

profile of v4, /device:TPU:31, one launch (start us, length us, event | category | flops | bytes accessed | tf_op | source)
XLA Modules:
  0.0 54.6 jit_solution(3823661801939998053)
XLA Ops:
  0.0 53.6 %shard_map.73 = bf16[256,2048]{1,0:T(8,128)(2,1)S(1)} custom-call(s32[4]{0:T(128)} %bitcast.14, f32[1,32]{1,0:T(1,128)} %bitcast.15, bf16[256,2048]{1,0:T(8,128)(2,1)} %bitcast.9, bf16[256,128]{1,0:T(8,128)(2,1)} %bitcast.10, bf16[256,128]{1,0:T(8,128)(2,1)} %bitcast.11, bf16[4,32,64]{2,1,0:T(8,128)(2,1)} %bitcast.12, bf16[4,32,64]{2,1,0:T(8,128)(2,1)} %bitcast.13), custom_call_target="tpu_custom_call" | custom-call | tf_op jit(solution)/shard_map/pallas_call | solution.py:442
  53.6 1.0 %copy.9 = bf16[4,64,2048]{2,1,0:T(8,128)(2,1)} copy(bf16[4,64,2048]{2,1,0:T(8,128)(2,1)S(1)} %bitcast.8) | data formatting | bytes 2097152

commit v5 on v4

--- a/solution.py
+++ b/solution.py
@@ -142,6 +142,12 @@
     col_ref,
     aux_out,
     aux_in,
+    help_in,
+    scores_out,
+    scores_in,
+    col_scores,
+    decay_out,
+    decay_in,
     sent,
     got,
     col_sent,
@@ -152,6 +158,9 @@
     load_sems,
     x_sems,
     aux_sems,
+    help_sems,
+    score_sems,
+    decay_sems,
     there_sems,
     back_sems,
     late_sem,
@@ -170,7 +179,9 @@
     def dot(a, b):
         return jnp.dot(a, b, preferred_element_type=f32)
 
-    quarter = devices // 4
+    quarter, half = devices // 4, devices // 2
+    middle = patches // 2
+    upper = me < half
     first = devices - quarter
     last = me >= first
     soon = jnp.where(last, devices - 1, first - 1)
@@ -296,7 +307,6 @@
             for r in range(tile_rows)
         ).astype(bf16)
 
-    aux_out[:, 2 * state :] = jnp.zeros((patches, aux_out.shape[1] - 2 * state), bf16)
     for load in loads[:4]:
         load.wait()
     tile = [mask_ref[r].astype(f32) for r in range(tile_rows)]
@@ -308,7 +318,22 @@
 
     aux_out[:, :state] = dot(order, keep(write_ref[...].astype(f32)).astype(bf16)).astype(bf16)
     aux_out[:, state : 2 * state] = dot(order, read_ref[...]).astype(bf16)
-    aux_out[:, 2 * state : 2 * state + heads] = turned(from_home, col_ref)
+    lanes = per * heads
+    groups = patches // per
+    lane_head = lax.broadcasted_iota(jnp.int32, (heads, lanes), 1) & (heads - 1)
+    copies = ones(lax.broadcasted_iota(jnp.int32, (heads, lanes), 0) == lane_head)
+    lane_col = shift(lax.broadcasted_iota(jnp.int32, (tile_cols, lanes), 1), heads)
+    kept = (lax.broadcasted_iota(jnp.int32, (tile_cols, lanes), 0) & (per - 1)) == lane_col
+    group = lax.broadcasted_iota(jnp.int32, (groups, tile_cols), 0)
+    group_col = lax.broadcasted_iota(jnp.int32, (groups, tile_cols), 1)
+    packed = jnp.zeros((groups, lanes), f32)
+    for r in range(tile_rows):
+        wide = lax.dot_general(
+            col_ref[r], copies, (((0,), (0,)), ((), ())), preferred_element_type=f32
+        )
+        wide = jnp.where(kept, wide, 0.0).astype(bf16)
+        packed += dot(ones(group == shift(group_col, per) * tile_rows + r), wide)
+    decay_out[...] = packed.astype(bf16).reshape(decay_out.shape)
 
     @pl.when(last)
     def _():
@@ -319,8 +344,50 @@
     def _():
         pl.semaphore_wait(barrier, first - 1)
 
-    scatter_soon(aux_out, aux_in, aux_sems)
+    def send_aux(other):
+        def rows(index):
+            return pl.ds(pl.multiple_of(index * block, block), block)
+
+        def copy(source, target, send_sem, recv_sem):
+            pltpu.make_async_remote_copy(
+                src_ref=source,
+                dst_ref=target,
+                send_sem=send_sem,
+                recv_sem=recv_sem,
+                device_id={"row": other},
+                device_id_type=MESH,
+            ).start()
+
+        above = other < half
+
+        @pl.when(jnp.logical_or(above, jnp.logical_not(upper)))
+        def _():
+            copy(aux_out.at[rows(other)], aux_in.at[own], aux_sems.at[0], aux_sems.at[1])
+
+        @pl.when(jnp.logical_and(above, upper))
+        def _():
+            copy(aux_out.at[rows(other + half)], help_in.at[own], help_sems.at[0], help_sems.at[1])
+
+        @pl.when(jnp.logical_and(above, jnp.logical_not(upper)))
+        def _():
+            copy(
+                aux_out.at[rows(other + half), pl.ds(state, state)],
+                help_in.at[own, pl.ds(state, state)],
+                help_sems.at[0],
+                help_sems.at[2],
+            )
+
+        copy(decay_out.at[other], decay_in.at[me], decay_sems.at[0], decay_sems.at[1])
+
+    each(soon, lambda step: send_aux(soon_peer(step)))
     aux_in[own, :] = aux_out[own, :]
+    decay_in[me] = decay_out[me]
+
+    @pl.when(upper)
+    def _():
+        twin = pl.ds(pl.multiple_of((me + half) * block, block), block)
+        help_in[own, :] = aux_out[twin, :]
+
 
     for c in range(chunks):
         x_loads[c].wait()
@@ -340,16 +407,17 @@
             @pl.when(jnp.logical_not(last))
             def _():
                 pl.semaphore_wait(late_sem, quarter)
-                scatter_late(aux_out, aux_in, aux_sems)
+                each(quarter, lambda step: send_aux(late_peer(step)))
                 scatter_late(sent.at[c], got.at[c], there_sems.at[c])
 
-    def spread(c):
-        head = lax.broadcasted_iota(jnp.int32, (heads, width), 0)
-        lane = lax.broadcasted_iota(jnp.int32, (heads, width), 1)
+    def spread(c, count=heads):
+        head = lax.broadcasted_iota(jnp.int32, (count, width), 0) & (heads - 1)
+        lane = lax.broadcasted_iota(jnp.int32, (count, width), 1)
         return (head == shift(lane + c * width, head_width)).astype(f32)
 
     def running(below, decays, c):
-        return dot(below, dot(decays, spread(c).astype(bf16)).astype(bf16))
+        own_head = spread(c, decays.shape[1]).astype(bf16)
+        return dot(below, dot(decays, own_head).astype(bf16))
 
     def products(reads, writes):
         return lax.dot_general(
@@ -358,6 +426,33 @@
 
     def causal(scores, allowed):
         return jnp.where(allowed, scores, 0.0).astype(bf16)
+
+    same_col = (down & (per - 1)) == (across & (per - 1))
+    earlier = (shift(down, block) > shift(across, block)) & same_col
+
+    fold = ones(lax.broadcasted_iota(jnp.int32, (groups, 1), 0) == shift(across, per))
+    slot = lax.broadcasted_iota(jnp.int32, (middle, middle), 0)
+    slot = (slot & (per - 1)) * (middle // per) + shift(slot, per)
+    swap = ones(slot == lax.broadcasted_iota(jnp.int32, (middle, middle), 1))
+
+    @pl.when(upper)
+    def _():
+        part = help_in.at[pl.ds(0, block * (half - 1))]
+        pltpu.make_async_copy(part, part, help_sems.at[1]).wait()
+        part = help_in.at[pl.ds(0, block * half), pl.ds(0, state)]
+        pltpu.make_async_copy(part, part, help_sems.at[2]).wait()
+        known = causal(
+            products(help_in[:, state:], help_in[:middle, :state]), earlier[:, :middle]
+        )
+        scores_out[...] = dot(fold, dot(known, swap).astype(bf16)).astype(bf16)
+        pltpu.make_async_remote_copy(
+            src_ref=scores_out,
+            dst_ref=scores_in,
+            send_sem=score_sems.at[0],
+            recv_sem=score_sems.at[1],
+            device_id={"row": me + half},
+            device_id_type=MESH,
+        ).start()
 
     restore = ones(down == home(across))
     in_row = (down >= across) & (shift(down, tile_cols) == shift(across, tile_cols))
@@ -383,20 +478,49 @@
         )[:1]
         total[:, cut] = jnp.exp(run) * dot(row_scores, faded) + gain * x_ref[:, cut].astype(f32)
 
-    same_col = (down & (per - 1)) == (across & (per - 1))
     col_below = ones((down >= across) & same_col)
-    wait(aux_in, aux_sems.at[1])
-    earlier = (shift(down, block) > shift(across, block)) & same_col
-    col_scores = causal(products(aux_in[:, state : 2 * state], aux_in[:, :state]), earlier)
+
+    @pl.when(upper)
+    def _():
+        wait(aux_in, aux_sems.at[1])
+        col_scores[...] = causal(products(aux_in[:, state:], aux_in[:, :state]), earlier)
+
+    @pl.when(jnp.logical_not(upper))
+    def _():
+        wait(aux_in, aux_sems.at[1], half - 1)
+        col_scores[:middle, middle:] = jnp.zeros((middle, middle), bf16)
+        col_scores[middle:, middle:] = causal(
+            products(aux_in[middle:, state:], aux_in[middle:, :state]), earlier[middle:, middle:]
+        )
+        pltpu.make_async_copy(scores_in, scores_in, score_sems.at[1]).wait()
+        wide = lax.dot_general(
+            fold, scores_in[...], (((0,), (0,)), ((), ())), preferred_element_type=f32
+        )
+        place = lax.broadcasted_iota(jnp.int32, (1, middle), 1)
+        wide = jnp.where(shift(place, middle // per) == (down & (per - 1)), wide, 0.0)
+        col_scores[:, :middle] = lax.dot_general(
+            wide.astype(bf16), swap, (((1,), (1,)), ((), ())), preferred_element_type=f32
+        ).astype(bf16)
+
+    pieces = decay_in.at[pl.ds(0, devices - 1)]
+    pltpu.make_async_copy(pieces, pieces, decay_sems.at[1]).wait()
+    wide = lax.dot_general(
+        fold,
+        decay_in[...].reshape(groups, lanes),
+        (((0,), (0,)), ((), ())),
+        preferred_element_type=f32,
+    )
+    place = lax.broadcasted_iota(jnp.int32, (1, lanes), 1)
+    col_decays = jnp.where(shift(place, heads) == (down & (per - 1)), wide, 0.0).astype(bf16)
     for c in range(chunks):
-        run = running(col_below, aux_in[:, 2 * state : 2 * state + heads], c)
+        run = running(col_below, col_decays, c)
         grow[c] = jnp.exp(run)
         fade[c] = jnp.exp(-run)
 
     for c in range(chunks):
         wait_either(got.at[c], there_sems.at[c, 1], tail)
         faded = (got[c].astype(f32) * fade[c]).astype(bf16)
-        col_sent[c] = (grow[c] * dot(col_scores, faded)).astype(bf16)
+        col_sent[c] = (grow[c] * dot(col_scores[...], faded)).astype(bf16)
         give_back(col_sent.at[c], col_got.at[c], back_sems.at[c])
         col_got[c, own, :] = col_sent[c, own, :]
         cut = slice(c * width, (c + 1) * width)
@@ -417,7 +541,20 @@
 
         out_ref[:, cut] = keep(total[:, cut] + dot(restore, col_got[c])).astype(bf16)
 
-    wait(aux_out, aux_sems.at[0])
+    pltpu.make_async_copy(pieces, pieces, decay_sems.at[0]).wait()
+
+    @pl.when(upper)
+    def _():
+        wait(aux_out, aux_sems.at[0], half - 1)
+        wait(aux_out, help_sems.at[0], half - 1)
+        pltpu.make_async_copy(scores_out, scores_out, score_sems.at[0]).wait()
+
+    @pl.when(jnp.logical_not(upper))
+    def _():
+        wait(aux_out, aux_sems.at[0])
+        part = help_in.at[pl.ds(0, block * half), pl.ds(0, state)]
+        pltpu.make_async_copy(part, part, help_sems.at[0]).wait()
+
     for c in range(chunks):
         wait_either(col_sent.at[c], back_sems.at[c, 0], head)
 
@@ -438,7 +575,10 @@
 
     vmem = pl.BlockSpec(memory_space=pltpu.VMEM)
     piece = (CHUNKS, patches, width)
-    aux = pltpu.VMEM((patches, 2 * state + 128), jnp.bfloat16)
+    aux = pltpu.VMEM((patches, 2 * state), jnp.bfloat16)
+    per = tile_cols // devices
+    scores = pltpu.VMEM((patches // per, patches // 2), jnp.bfloat16)
+    decays = pltpu.VMEM((devices, tile_rows, per * heads), jnp.bfloat16)
     result = pl.pallas_call(
         functools.partial(fused_kernel, (devices, tile_rows, tile_cols, heads)),
         out_shape=pltpu.VMEM((patches, span_width), jnp.bfloat16),
@@ -454,6 +594,12 @@
             pltpu.VMEM((tile_rows, heads, tile_cols), jnp.bfloat16),
             aux,
             aux,
+            aux,
+            scores,
+            scores,
+            pltpu.VMEM((patches, patches), jnp.bfloat16),
+            decays,
+            decays,
             pltpu.VMEM(piece, jnp.bfloat16),
             pltpu.VMEM(piece, jnp.bfloat16),
             pltpu.VMEM(piece, jnp.bfloat16),
@@ -463,6 +609,9 @@
             pltpu.VMEM(piece, jnp.float32),
             pltpu.SemaphoreType.DMA((6,)),
             pltpu.SemaphoreType.DMA((CHUNKS,)),
+            pltpu.SemaphoreType.DMA((2,)),
+            pltpu.SemaphoreType.DMA((3,)),
+            pltpu.SemaphoreType.DMA((2,)),
             pltpu.SemaphoreType.DMA((2,)),
             pltpu.SemaphoreType.DMA((CHUNKS, 2)),
             pltpu.SemaphoreType.DMA((CHUNKS, 2)),
@@ -494,7 +643,8 @@
         and tile_cols <= 64
         and (tile_rows * (tile_cols // devices)) % 16 == 0
         and span_width % (CHUNKS * 128) == 0
-        and row_decay.shape[-1] <= 128
+        and (tile_cols // devices) * row_decay.shape[-1] == 128
+        and tile_rows * tile_cols % 256 == 0
         and all(
             size.bit_count() == 1
             for size in (tile_rows, tile_cols, devices, span_width // row_decay.shape[-1])

time: 54.7 us -> 56.4 us (1.031)
  the two profiles are of different devices: /device:TPU:31 before, /device:TPU:1 now
where the time goes in v5:
time: 56.4 us; the launch traced here: 56.2 us
  Pallas kernels  55.3 us (98%)
  local copies, waits for them, and re-layouts  0.97 us (2%)
    pallas_call x1, Pallas kernels, fused(): pl.pallas_call(functools.partial(fused_kernel, (devices, tile_rows, tile_...  55.3 us

profile of v5, /device:TPU:1, one launch (start us, length us, event | category | flops | bytes accessed | tf_op | source)
XLA Modules:
  0.0 56.2 jit_solution(989620631512715605)
XLA Ops:
  0.0 55.3 %shard_map.73 = bf16[256,2048]{1,0:T(8,128)(2,1)S(1)} custom-call(s32[4]{0:T(128)} %bitcast.14, f32[1,32]{1,0:T(1,128)} %bitcast.15, bf16[256,2048]{1,0:T(8,128)(2,1)} %bitcast.9, bf16[256,128]{1,0:T(8,128)(2,1)} %bitcast.10, bf16[256,128]{1,0:T(8,128)(2,1)} %bitcast.11, bf16[4,32,64]{2,1,0:T(8,128)(2,1)} %bitcast.12, bf16[4,32,64]{2,1,0:T(8,128)(2,1)} %bitcast.13), custom_call_target="tpu_custom_call" | custom-call | tf_op jit(solution)/shard_map/pallas_call | solution.py:582
  55.3 1.0 %copy.9 = bf16[4,64,2048]{2,1,0:T(8,128)(2,1)} copy(bf16[4,64,2048]{2,1,0:T(8,128)(2,1)S(1)} %bitcast.8) | data formatting | bytes 2097152

commit v6 on v5

--- a/solution.py
+++ b/solution.py
@@ -389,36 +389,6 @@
         help_in[own, :] = aux_out[twin, :]
 
 
-    for c in range(chunks):
-        x_loads[c].wait()
-        sent[c] = dot(order, x_ref[:, c * width : (c + 1) * width]).astype(bf16)
-        got[c, block * (devices - 1) :, :] = jnp.zeros((block, width), bf16)
-        got[c, own, :] = sent[c, own, :]
-
-        @pl.when(jnp.logical_not(tail))
-        def _():
-            if c:
-                each(devices - 1, lambda step: send(sent.at[c], got.at[c], there_sems.at[c], peer(step)))
-            else:
-                scatter_soon(sent.at[c], got.at[c], there_sems.at[c])
-
-        if not c:
-
-            @pl.when(jnp.logical_not(last))
-            def _():
-                pl.semaphore_wait(late_sem, quarter)
-                each(quarter, lambda step: send_aux(late_peer(step)))
-                scatter_late(sent.at[c], got.at[c], there_sems.at[c])
-
-    def spread(c, count=heads):
-        head = lax.broadcasted_iota(jnp.int32, (count, width), 0) & (heads - 1)
-        lane = lax.broadcasted_iota(jnp.int32, (count, width), 1)
-        return (head == shift(lane + c * width, head_width)).astype(f32)
-
-    def running(below, decays, c):
-        own_head = spread(c, decays.shape[1]).astype(bf16)
-        return dot(below, dot(decays, own_head).astype(bf16))
-
     def products(reads, writes):
         return lax.dot_general(
             reads, writes, (((1,), (1,)), ((), ())), preferred_element_type=f32
@@ -435,8 +405,7 @@
     slot = (slot & (per - 1)) * (middle // per) + shift(slot, per)
     swap = ones(slot == lax.broadcasted_iota(jnp.int32, (middle, middle), 1))
 
-    @pl.when(upper)
-    def _():
+    def help_below():
         part = help_in.at[pl.ds(0, block * (half - 1))]
         pltpu.make_async_copy(part, part, help_sems.at[1]).wait()
         part = help_in.at[pl.ds(0, block * half), pl.ds(0, state)]
@@ -453,6 +422,42 @@
             device_id={"row": me + half},
             device_id_type=MESH,
         ).start()
+
+    for c in range(chunks):
+        x_loads[c].wait()
+        sent[c] = dot(order, x_ref[:, c * width : (c + 1) * width]).astype(bf16)
+        got[c, block * (devices - 1) :, :] = jnp.zeros((block, width), bf16)
+        got[c, own, :] = sent[c, own, :]
+
+        @pl.when(jnp.logical_not(tail))
+        def _():
+            if c:
+                each(devices - 1, lambda step: send(sent.at[c], got.at[c], there_sems.at[c], peer(step)))
+            else:
+                scatter_soon(sent.at[c], got.at[c], there_sems.at[c])
+
+        if not c:
+
+            @pl.when(jnp.logical_not(last))
+            def _():
+                pl.semaphore_wait(late_sem, quarter)
+                each(quarter, lambda step: send_aux(late_peer(step)))
+                scatter_late(sent.at[c], got.at[c], there_sems.at[c])
+
+        if c == 1:
+
+            @pl.when(upper)
+            def _():
+                help_below()
+
+    def spread(c, count=heads):
+        head = lax.broadcasted_iota(jnp.int32, (count, width), 0) & (heads - 1)
+        lane = lax.broadcasted_iota(jnp.int32, (count, width), 1)
+        return (head == shift(lane + c * width, head_width)).astype(f32)
+
+    def running(below, decays, c):
+        own_head = spread(c, decays.shape[1]).astype(bf16)
+        return dot(below, dot(decays, own_head).astype(bf16))
 
     restore = ones(down == home(across))
     in_row = (down >= across) & (shift(down, tile_cols) == shift(across, tile_cols))

time: 56.4 us -> 52.7 us (0.934)
  the two profiles are of different devices: /device:TPU:1 before, /device:TPU:31 now
where the time goes in v6:
time: 52.7 us; the launch traced here: 52.3 us
  Pallas kernels  51.3 us (97%)
  local copies, waits for them, and re-layouts  0.97 us (2%)
    pallas_call x1, Pallas kernels, fused(): pl.pallas_call(functools.partial(fused_kernel, (devices, tile_rows, tile_...  51.3 us

profile of v6, /device:TPU:31, one launch (start us, length us, event | category | flops | bytes accessed | tf_op | source)
XLA Modules:
  0.0 52.3 jit_solution(17987234829544436692)
XLA Ops:
  0.0 51.3 %shard_map.73 = bf16[256,2048]{1,0:T(8,128)(2,1)S(1)} custom-call(s32[4]{0:T(128)} %bitcast.14, f32[1,32]{1,0:T(1,128)} %bitcast.15, bf16[256,2048]{1,0:T(8,128)(2,1)} %bitcast.9, bf16[256,128]{1,0:T(8,128)(2,1)} %bitcast.10, bf16[256,128]{1,0:T(8,128)(2,1)} %bitcast.11, bf16[4,32,64]{2,1,0:T(8,128)(2,1)} %bitcast.12, bf16[4,32,64]{2,1,0:T(8,128)(2,1)} %bitcast.13), custom_call_target="tpu_custom_call" | custom-call | tf_op jit(solution)/shard_map/pallas_call | solution.py:587
  51.3 1.0 %copy.9 = bf16[4,64,2048]{2,1,0:T(8,128)(2,1)} copy(bf16[4,64,2048]{2,1,0:T(8,128)(2,1)S(1)} %bitcast.8) | data formatting | bytes 2097152

commit v7 on v6

--- a/solution.py
+++ b/solution.py
@@ -148,6 +148,10 @@
     col_scores,
     decay_out,
     decay_in,
+    pair_x,
+    pair_write,
+    pair_col,
+    kept_write,
     sent,
     got,
     col_sent,
@@ -161,6 +165,7 @@
     help_sems,
     score_sems,
     decay_sems,
+    pair_sems,
     there_sems,
     back_sems,
     late_sem,
@@ -247,8 +252,9 @@
             device_id_type=MESH,
         ).start()
 
-    tail = me == devices - 1
-    head = me == 0
+    tail = me >= devices - 2
+    head = me < 2
+    odd = (me & 1) == 1
 
     def scatter_soon(source, target, sems):
         each(soon, lambda step: send(source, target, sems, soon_peer(step)))
@@ -260,7 +266,7 @@
         def act(step):
             other = peer(step)
 
-            @pl.when(other != 0)
+            @pl.when(other >= 2)
             def _():
                 send(source, target, sems, other)
 
@@ -270,14 +276,16 @@
         part = buffer.at[pl.ds(0, block * count)]
         pltpu.make_async_copy(part, part, sem).wait()
 
-    def wait_either(buffer, sem, all_of_them):
-        @pl.when(all_of_them)
-        def _():
-            wait(buffer, sem)
-
-        @pl.when(jnp.logical_not(all_of_them))
+    def wait_either(buffer, sem, one_more):
+        @pl.when(one_more)
         def _():
             wait(buffer, sem, devices - 2)
+
+        @pl.when(jnp.logical_not(one_more))
+        def _():
+            wait(buffer, sem, devices - 3)
+
+    pairs = [(x_ref, pair_x), (kept_write, pair_write), (col_ref, pair_col)]
 
     def shift(i, size):
         return lax.shift_right_logical(i, size.bit_length() - 1)
@@ -307,6 +315,22 @@
             for r in range(tile_rows)
         ).astype(bf16)
 
+    x_loads[0].wait()
+    sent[0] = dot(order, x_ref[:, :width]).astype(bf16)
+
+    @pl.when(last)
+    def _():
+        pl.semaphore_wait(barrier, devices - 1)
+        each(first, lambda step: greet(lax.rem(me + step, first), late_sem))
+
+    @pl.when(jnp.logical_not(last))
+    def _():
+        pl.semaphore_wait(barrier, first - 1)
+
+    @pl.when(jnp.logical_not(tail))
+    def _():
+        scatter_soon(sent.at[0], got.at[0], there_sems.at[0])
+
     for load in loads[:4]:
         load.wait()
     tile = [mask_ref[r].astype(f32) for r in range(tile_rows)]
@@ -316,7 +340,8 @@
             [value[r * tile_cols : (r + 1) * tile_cols] * tile[r] for r in range(tile_rows)]
         )
 
-    aux_out[:, :state] = dot(order, keep(write_ref[...].astype(f32)).astype(bf16)).astype(bf16)
+    kept_write[...] = keep(write_ref[...].astype(f32)).astype(bf16)
+    aux_out[:, :state] = dot(order, kept_write[...]).astype(bf16)
     aux_out[:, state : 2 * state] = dot(order, read_ref[...]).astype(bf16)
     lanes = per * heads
     groups = patches // per
@@ -335,15 +360,6 @@
         packed += dot(ones(group == shift(group_col, per) * tile_rows + r), wide)
     decay_out[...] = packed.astype(bf16).reshape(decay_out.shape)
 
-    @pl.when(last)
-    def _():
-        pl.semaphore_wait(barrier, devices - 1)
-        each(first, lambda step: greet(lax.rem(me + step, first), late_sem))
-
-    @pl.when(jnp.logical_not(last))
-    def _():
-        pl.semaphore_wait(barrier, first - 1)
-
     def send_aux(other):
         def rows(index):
             return pl.ds(pl.multiple_of(index * block, block), block)
@@ -398,7 +414,7 @@
         return jnp.where(allowed, scores, 0.0).astype(bf16)
 
     same_col = (down & (per - 1)) == (across & (per - 1))
-    earlier = (shift(down, block) > shift(across, block)) & same_col
+    earlier = (shift(down, 2 * block) > shift(across, 2 * block)) & same_col
 
     fold = ones(lax.broadcasted_iota(jnp.int32, (groups, 1), 0) == shift(across, per))
     slot = lax.broadcasted_iota(jnp.int32, (middle, middle), 0)
@@ -424,19 +440,19 @@
         ).start()
 
     for c in range(chunks):
-        x_loads[c].wait()
-        sent[c] = dot(order, x_ref[:, c * width : (c + 1) * width]).astype(bf16)
-        got[c, block * (devices - 1) :, :] = jnp.zeros((block, width), bf16)
+        if c:
+            x_loads[c].wait()
+            sent[c] = dot(order, x_ref[:, c * width : (c + 1) * width]).astype(bf16)
+        got[c, block * (devices - 2) :, :] = jnp.zeros((2 * block, width), bf16)
         got[c, own, :] = sent[c, own, :]
 
-        @pl.when(jnp.logical_not(tail))
-        def _():
-            if c:
+        if c:
+
+            @pl.when(jnp.logical_not(tail))
+            def _():
                 each(devices - 1, lambda step: send(sent.at[c], got.at[c], there_sems.at[c], peer(step)))
-            else:
-                scatter_soon(sent.at[c], got.at[c], there_sems.at[c])
-
-        if not c:
+
+        else:
 
             @pl.when(jnp.logical_not(last))
             def _():
@@ -444,11 +460,23 @@
                 each(quarter, lambda step: send_aux(late_peer(step)))
                 scatter_late(sent.at[c], got.at[c], there_sems.at[c])
 
-        if c == 1:
+        if c == 2:
 
             @pl.when(upper)
             def _():
                 help_below()
+
+    @pl.when(jnp.logical_not(odd))
+    def _():
+        for i, (source, target) in enumerate(pairs):
+            pltpu.make_async_remote_copy(
+                src_ref=source,
+                dst_ref=target,
+                send_sem=pair_sems.at[i, 0],
+                recv_sem=pair_sems.at[i, 1],
+                device_id={"row": me + 1},
+                device_id_type=MESH,
+            ).start()
 
     def spread(c, count=heads):
         head = lax.broadcasted_iota(jnp.int32, (count, width), 0) & (heads - 1)
@@ -528,10 +556,32 @@
         col_sent[c] = (grow[c] * dot(col_scores[...], faded)).astype(bf16)
         give_back(col_sent.at[c], col_got.at[c], back_sems.at[c])
         col_got[c, own, :] = col_sent[c, own, :]
+
+    for c in range(chunks):
         cut = slice(c * width, (c + 1) * width)
         run = running(home_below, home_decays, c)
+        grow[c] = jnp.exp(run)
         faded = (x_ref[:, cut].astype(f32) * jnp.exp(-run)).astype(bf16)
-        total[:, cut] += jnp.exp(run) * dot(home_scores, faded)
+        total[:, cut] += grow[c] * dot(home_scores, faded)
+
+    @pl.when(odd)
+    def _():
+        for i, (source, target) in enumerate(pairs):
+            pltpu.make_async_copy(target, target, pair_sems.at[i, 1]).wait()
+        alike = (down & (tile_cols - 1)) == (across & (tile_cols - 1))
+        pair_after = ones((shift(down, tile_cols) < shift(across, tile_cols)) & alike)
+        pair_decays = turned(down, pair_col)
+        pair_scores = causal(products(read_ref[...], pair_write[...]), alike)
+        for c in range(chunks):
+            cut = slice(c * width, (c + 1) * width)
+            run = running(pair_after, pair_decays, c)
+            faded = (pair_x[:, cut].astype(f32) * jnp.exp(run)).astype(bf16)
+            total[:, cut] += grow[c] * dot(pair_scores, faded)
+
+    @pl.when(jnp.logical_not(odd))
+    def _():
+        for i, (source, target) in enumerate(pairs):
+            pltpu.make_async_copy(source, source, pair_sems.at[i, 0]).wait()
 
     for c in range(chunks):
         cut = slice(c * width, (c + 1) * width)
@@ -605,6 +655,10 @@
             pltpu.VMEM((patches, patches), jnp.bfloat16),
             decays,
             decays,
+            pltpu.VMEM((patches, span_width), jnp.bfloat16),
+            pltpu.VMEM((patches, state), jnp.bfloat16),
+            pltpu.VMEM((tile_rows, heads, tile_cols), jnp.bfloat16),
+            pltpu.VMEM((patches, state), jnp.bfloat16),
             pltpu.VMEM(piece, jnp.bfloat16),
             pltpu.VMEM(piece, jnp.bfloat16),
             pltpu.VMEM(piece, jnp.bfloat16),
@@ -618,6 +672,7 @@
             pltpu.SemaphoreType.DMA((3,)),
             pltpu.SemaphoreType.DMA((2,)),
             pltpu.SemaphoreType.DMA((2,)),
+            pltpu.SemaphoreType.DMA((3, 2)),
             pltpu.SemaphoreType.DMA((CHUNKS, 2)),
             pltpu.SemaphoreType.DMA((CHUNKS, 2)),
             pltpu.SemaphoreType.REGULAR,

time: 52.7 us -> 52.3 us (level)
  no operation moved by 1% of the time
where the time goes in v7:
time: 52.3 us; the launch traced here: 52.2 us
  Pallas kernels  51.2 us (98%)
  local copies, waits for them, and re-layouts  0.97 us (2%)
    pallas_call x1, Pallas kernels, fused(): pl.pallas_call(functools.partial(fused_kernel, (devices, tile_rows, tile_...  51.2 us

profile of v7, /device:TPU:31, one launch (start us, length us, event | category | flops | bytes accessed | tf_op | source)
XLA Modules:
  0.0 52.2 jit_solution(4925330074229405639)
XLA Ops:
  0.0 51.2 %shard_map.73 = bf16[256,2048]{1,0:T(8,128)(2,1)S(1)} custom-call(s32[4]{0:T(128)} %bitcast.14, f32[1,32]{1,0:T(1,128)} %bitcast.15, bf16[256,2048]{1,0:T(8,128)(2,1)} %bitcast.9, bf16[256,128]{1,0:T(8,128)(2,1)} %bitcast.10, bf16[256,128]{1,0:T(8,128)(2,1)} %bitcast.11, bf16[4,32,64]{2,1,0:T(8,128)(2,1)} %bitcast.12, bf16[4,32,64]{2,1,0:T(8,128)(2,1)} %bitcast.13), custom_call_target="tpu_custom_call" | custom-call | tf_op jit(solution)/shard_map/pallas_call | solution.py:637
  51.2 1.0 %copy.9 = bf16[4,64,2048]{2,1,0:T(8,128)(2,1)} copy(bf16[4,64,2048]{2,1,0:T(8,128)(2,1)S(1)} %bitcast.8) | data formatting | bytes 2097152

commit v8 on v7

--- a/solution.py
+++ b/solution.py
@@ -218,7 +218,7 @@
 
     @pl.when(jnp.logical_not(last))
     def _():
-        each(devices - 1, lambda step: greet(peer(step)))
+        each(devices - 1, lambda step: greet(lax.rem(me - 1 - step + devices, devices)))
 
     loads = [
         pltpu.make_async_copy(source, target, load_sems.at[i])
@@ -321,7 +321,7 @@
     @pl.when(last)
     def _():
         pl.semaphore_wait(barrier, devices - 1)
-        each(first, lambda step: greet(lax.rem(me + step, first), late_sem))
+        each(first, lambda step: greet(first - 1 - lax.rem(me + step, first), late_sem))
 
     @pl.when(jnp.logical_not(last))
     def _():

time: 52.3 us -> 52.2 us (level)
  no operation moved by 1% of the time
where the time goes in v8:
time: 52.2 us; the launch traced here: 52.1 us
  Pallas kernels  51.1 us (98%)
  local copies, waits for them, and re-layouts  0.97 us (2%)
    pallas_call x1, Pallas kernels, fused(): pl.pallas_call(functools.partial(fused_kernel, (devices, tile_rows, tile_...  51.1 us

profile of v8, /device:TPU:31, one launch (start us, length us, event | category | flops | bytes accessed | tf_op | source)
XLA Modules:
  0.0 52.1 jit_solution(8381732193288999545)
XLA Ops:
  0.0 51.1 %shard_map.73 = bf16[256,2048]{1,0:T(8,128)(2,1)S(1)} custom-call(s32[4]{0:T(128)} %bitcast.14, f32[1,32]{1,0:T(1,128)} %bitcast.15, bf16[256,2048]{1,0:T(8,128)(2,1)} %bitcast.9, bf16[256,128]{1,0:T(8,128)(2,1)} %bitcast.10, bf16[256,128]{1,0:T(8,128)(2,1)} %bitcast.11, bf16[4,32,64]{2,1,0:T(8,128)(2,1)} %bitcast.12, bf16[4,32,64]{2,1,0:T(8,128)(2,1)} %bitcast.13), custom_call_target="tpu_custom_call" | custom-call | tf_op jit(solution)/shard_map/pallas_call | solution.py:637
  51.1 1.0 %copy.9 = bf16[4,64,2048]{2,1,0:T(8,128)(2,1)} copy(bf16[4,64,2048]{2,1,0:T(8,128)(2,1)S(1)} %bitcast.8) | data formatting | bytes 2097152

commit v9 on v8

--- a/solution.py
+++ b/solution.py
@@ -195,7 +195,16 @@
         return lax.rem(me + 1 + step, devices)
 
     def soon_peer(step):
-        return lax.rem(me + 1 + step, soon + 1)
+        across_first = jnp.where(
+            step < quarter, half + lax.rem(me + step, quarter), lax.rem(me + 1 + step - quarter, half)
+        )
+        return jnp.where(upper, across_first, lax.rem(me + 1 + step, soon + 1))
+
+    def far_peer(step):
+        across_first = jnp.where(
+            step < half, half + lax.rem(me + step, half), lax.rem(me + 1 + step - half, half)
+        )
+        return jnp.where(upper, across_first, peer(step))
 
     def late_peer(step):
         return first + lax.rem(me + step, quarter)
@@ -450,7 +459,7 @@
 
             @pl.when(jnp.logical_not(tail))
             def _():
-                each(devices - 1, lambda step: send(sent.at[c], got.at[c], there_sems.at[c], peer(step)))
+                each(devices - 1, lambda step: send(sent.at[c], got.at[c], there_sems.at[c], far_peer(step)))
 
         else:
 
@@ -487,7 +496,7 @@
         own_head = spread(c, decays.shape[1]).astype(bf16)
         return dot(below, dot(decays, own_head).astype(bf16))
 
-    restore = ones(down == home(across))
+    restore = keep((down == home(across)).astype(f32)).astype(bf16)
     in_row = (down >= across) & (shift(down, tile_cols) == shift(across, tile_cols))
     row_below = ones(in_row)
     for load in loads[4:]:
@@ -583,6 +592,7 @@
         for i, (source, target) in enumerate(pairs):
             pltpu.make_async_copy(source, source, pair_sems.at[i, 0]).wait()
 
+    total[...] = keep(total[...])
     for c in range(chunks):
         cut = slice(c * width, (c + 1) * width)
 
@@ -594,7 +604,7 @@
         def _():
             wait(col_got.at[c], back_sems.at[c, 1])
 
-        out_ref[:, cut] = keep(total[:, cut] + dot(restore, col_got[c])).astype(bf16)
+        out_ref[:, cut] = (total[:, cut] + dot(restore, col_got[c])).astype(bf16)
 
     pltpu.make_async_copy(pieces, pieces, decay_sems.at[0]).wait()
 

time: 52.2 us -> 51.7 us (level)
  Pallas kernels: 51.1 us -> 50.5 us
    pallas_call x1, Pallas kernels: 51.1 us -> 50.5 us  [fused(): pl.pallas_call(functools.partial(fused_kernel, (devices, tile_rows, tile_...]
where the time goes in v9:
time: 51.7 us; the launch traced here: 51.5 us
  Pallas kernels  50.5 us (98%)
  local copies, waits for them, and re-layouts  0.97 us (2%)
    pallas_call x1, Pallas kernels, fused(): pl.pallas_call(functools.partial(fused_kernel, (devices, tile_rows, tile_...  50.5 us

profile of v9, /device:TPU:31, one launch (start us, length us, event | category | flops | bytes accessed | tf_op | source)
XLA Modules:
  0.0 51.5 jit_solution(7909267035120523388)
XLA Ops:
  0.0 50.5 %shard_map.73 = bf16[256,2048]{1,0:T(8,128)(2,1)S(1)} custom-call(s32[4]{0:T(128)} %bitcast.14, f32[1,32]{1,0:T(1,128)} %bitcast.15, bf16[256,2048]{1,0:T(8,128)(2,1)} %bitcast.9, bf16[256,128]{1,0:T(8,128)(2,1)} %bitcast.10, bf16[256,128]{1,0:T(8,128)(2,1)} %bitcast.11, bf16[4,32,64]{2,1,0:T(8,128)(2,1)} %bitcast.12, bf16[4,32,64]{2,1,0:T(8,128)(2,1)} %bitcast.13), custom_call_target="tpu_custom_call" | custom-call | tf_op jit(solution)/shard_map/pallas_call | solution.py:647
  50.5 1.0 %copy.9 = bf16[4,64,2048]{2,1,0:T(8,128)(2,1)} copy(bf16[4,64,2048]{2,1,0:T(8,128)(2,1)S(1)} %bitcast.8) | data formatting | bytes 2097152

commit v10 on v9

--- a/solution.py
+++ b/solution.py
@@ -121,6 +121,7 @@
 
 MESH = pl.DeviceIdType.MESH
 CHUNKS = 4
+PIECES = 2
 
 
 def fused_kernel(
@@ -133,6 +134,9 @@
     row_hbm,
     col_hbm,
     out_ref,
+    rest_ref,
+    final_ref,
+    restore_ref,
     mask_ref,
     skip_ref,
     x_ref,
@@ -592,9 +596,33 @@
         for i, (source, target) in enumerate(pairs):
             pltpu.make_async_copy(source, source, pair_sems.at[i, 0]).wait()
 
+    pltpu.make_async_copy(pieces, pieces, decay_sems.at[0]).wait()
+
+    @pl.when(upper)
+    def _():
+        wait(aux_out, aux_sems.at[0], half - 1)
+        wait(aux_out, help_sems.at[0], half - 1)
+        pltpu.make_async_copy(scores_out, scores_out, score_sems.at[0]).wait()
+
+    @pl.when(jnp.logical_not(upper))
+    def _():
+        wait(aux_out, aux_sems.at[0])
+        part = help_in.at[pl.ds(0, block * half), pl.ds(0, state)]
+        pltpu.make_async_copy(part, part, help_sems.at[0]).wait()
+
+    @pl.when(jnp.logical_not(tail))
+    def _():
+        for c in range(chunks):
+            wait(sent.at[c], there_sems.at[c, 0])
+
     total[...] = keep(total[...])
+    rest_ref[...] = total[:, (chunks - 1) * width :]
+    restore_ref[...] = restore
     for c in range(chunks):
         cut = slice(c * width, (c + 1) * width)
+
+        if c:
+            wait_either(col_sent.at[c - 1], back_sems.at[c - 1, 0], head)
 
         @pl.when(head)
         def _():
@@ -604,28 +632,32 @@
         def _():
             wait(col_got.at[c], back_sems.at[c, 1])
 
-        out_ref[:, cut] = (total[:, cut] + dot(restore, col_got[c])).astype(bf16)
-
-    pltpu.make_async_copy(pieces, pieces, decay_sems.at[0]).wait()
-
-    @pl.when(upper)
-    def _():
-        wait(aux_out, aux_sems.at[0], half - 1)
-        wait(aux_out, help_sems.at[0], half - 1)
-        pltpu.make_async_copy(scores_out, scores_out, score_sems.at[0]).wait()
-
-    @pl.when(jnp.logical_not(upper))
-    def _():
-        wait(aux_out, aux_sems.at[0])
-        part = help_in.at[pl.ds(0, block * half), pl.ds(0, state)]
-        pltpu.make_async_copy(part, part, help_sems.at[0]).wait()
-
-    for c in range(chunks):
-        wait_either(col_sent.at[c], back_sems.at[c, 0], head)
-
-        @pl.when(jnp.logical_not(tail))
-        def _():
-            wait(sent.at[c], there_sems.at[c, 0])
+        if c == chunks - 1:
+            final_ref[...] = col_got[c]
+        else:
+            out_ref[:, cut] = (total[:, cut] + dot(restore, col_got[c])).astype(bf16)
+
+    wait_either(col_sent.at[chunks - 1], back_sems.at[chunks - 1, 0], head)
+
+
+def finish_kernel(done, rest, final, restore, out_hbm, last, sems):
+    patches, width = final.shape
+    ready = done.shape[1]
+    rows = patches // PIECES
+    copies = [pltpu.make_async_copy(done, out_hbm.at[:, pl.ds(0, ready)], sems.at[PIECES])]
+    copies[0].start()
+    for i in range(PIECES):
+        part = pl.ds(i * rows, rows)
+        back = jnp.dot(restore[part, :], final[...], preferred_element_type=jnp.float32)
+        last[part, :] = (rest[part, :] + back).astype(jnp.bfloat16)
+        copies.append(
+            pltpu.make_async_copy(
+                last.at[part], out_hbm.at[part, pl.ds(ready, width)], sems.at[i]
+            )
+        )
+        copies[-1].start()
+    for copy in copies:
+        copy.wait()
 
 
 def fused(features, write_vecs, read_vecs, row_decay, col_decay, tile_mask, skip_gain):
@@ -646,9 +678,14 @@
     decays = pltpu.VMEM((devices, tile_rows, per * heads), jnp.bfloat16)
     result = pl.pallas_call(
         functools.partial(fused_kernel, (devices, tile_rows, tile_cols, heads)),
-        out_shape=pltpu.VMEM((patches, span_width), jnp.bfloat16),
+        out_shape=(
+            pltpu.VMEM((patches, span_width - width), jnp.bfloat16),
+            pltpu.VMEM((patches, width), jnp.float32),
+            pltpu.VMEM((patches, width), jnp.bfloat16),
+            pltpu.VMEM((patches, patches), jnp.bfloat16),
+        ),
         in_specs=[pl.BlockSpec(memory_space=pl.ANY)] * 7,
-        out_specs=vmem,
+        out_specs=(vmem,) * 4,
         scratch_shapes=[
             pltpu.SMEM((tile_rows,), jnp.int32),
             pltpu.VMEM((1, heads), jnp.float32),
@@ -699,7 +736,17 @@
         jnp.swapaxes(row_decay, 1, 2),
         jnp.swapaxes(col_decay, 1, 2),
     )
-    return result.reshape(features.shape)
+    stored = pl.pallas_call(
+        finish_kernel,
+        out_shape=jax.ShapeDtypeStruct((patches, span_width), jnp.bfloat16),
+        in_specs=[vmem] * 4,
+        out_specs=pl.BlockSpec(memory_space=pl.ANY),
+        scratch_shapes=[
+            pltpu.VMEM((patches, width), jnp.bfloat16),
+            pltpu.SemaphoreType.DMA((PIECES + 1,)),
+        ],
+    )(*(pltpu.with_memory_space_constraint(part, pltpu.VMEM) for part in result))
+    return stored.reshape(features.shape)
 
 
 def fits_fused(features, row_decay, tile_mask):

time: 51.7 us -> 51.5 us (level)
  local copies, waits for them, and re-layouts: 0.97 us -> 0 us
  Pallas kernels: 50.5 us -> 51.3 us
    pallas_call x0 -> x1, Pallas kernels: none -> 1 us  [fused(): pl.pallas_call(finish_kernel, out_shape=jax.ShapeDtypeStruct((patches, sp...]
    unnamed x1 -> x0, local copies, waits for them, and re-layouts: 0.97 us -> none
where the time goes in v10:
time: 51.5 us; the launch traced here: 51.3 us
  Pallas kernels  51.3 us (100%)
    pallas_call x1, Pallas kernels, fused(): pl.pallas_call(functools.partial(fused_kernel, (devices, tile_rows, tile_...  50.3 us

profile of v10, /device:TPU:31, one launch (start us, length us, event | category | flops | bytes accessed | tf_op | source)
XLA Modules:
  0.0 51.3 jit_solution(14295792467325541158)
XLA Ops:
  0.0 50.3 %shard_map.73 = (bf16[256,1536]{1,0:T(8,128)(2,1)S(1)}, f32[256,512]{1,0:T(8,128)S(1)}, bf16[256,512]{1,0:T(8,128)(2,1)S(1)}, bf16[256,256]{1,0:T(8,128)(2,1)S(1)}) custom-call(s32[4]{0:T(128)} %bitcast.13, f32[1,32]{1,0:T(1,128)} %bitcast.14, bf16[256,2048]{1,0:T(8,128)(2,1)} %bitcast.8, bf16[256,128]{1,0:T(8,128)(2,1)} %bitcast.9, ...), custom_call_target="tpu_custom_call" | custom-call | tf_op jit(solution)/shard_map/pallas_call | solution.py:679
  50.3 1.0 %shard_map.74 = bf16[256,2048]{1,0:T(8,128)(2,1)} custom-call(bf16[256,1536]{1,0:T(8,128)(2,1)S(1)} %get-tuple-element.9.done, f32[256,512]{1,0:T(8,128)S(1)} %get-tuple-element.10.rest, bf16[256,512]{1,0:T(8,128)(2,1)S(1)} %get-tuple-element.11.final, bf16[256,256]{1,0:T(8,128)(2,1)S(1)} %get-tuple-element.12.restore), custom_call_target="tpu_custom_call" | custom-call | tf_op jit(solution)/shard_map/pallas_call | solution.py:739

commit v11 on v10

--- a/solution.py
+++ b/solution.py
@@ -121,7 +121,7 @@
 
 MESH = pl.DeviceIdType.MESH
 CHUNKS = 4
-PIECES = 2
+PIECES = 1
 
 
 def fused_kernel(
@@ -259,8 +259,8 @@
         pltpu.make_async_remote_copy(
             src_ref=source.at[pl.ds(pl.multiple_of(other * block, block), block)],
             dst_ref=target.at[own],
-            send_sem=sems.at[0],
-            recv_sem=sems.at[1],
+            send_sem=sems[0],
+            recv_sem=sems[1],
             device_id={"row": other},
             device_id_type=MESH,
         ).start()
@@ -274,6 +274,9 @@
 
     def scatter_late(source, target, sems):
         each(quarter, lambda step: send(source, target, sems, late_peer(step)))
+
+    def landing(c):
+        return final_ref if c == chunks - 1 else col_got.at[c]
 
     def give_back(source, target, sems):
         def act(step):
@@ -342,7 +345,7 @@
 
     @pl.when(jnp.logical_not(tail))
     def _():
-        scatter_soon(sent.at[0], got.at[0], there_sems.at[0])
+        scatter_soon(sent.at[0], got.at[0], (x_sems.at[0], there_sems.at[0]))
 
     for load in loads[:4]:
         load.wait()
@@ -434,6 +437,13 @@
     slot = (slot & (per - 1)) * (middle // per) + shift(slot, per)
     swap = ones(slot == lax.broadcasted_iota(jnp.int32, (middle, middle), 1))
 
+    two = groups // half
+    span = middle // per
+    lane_from = lax.broadcasted_iota(jnp.int32, (middle, middle), 0)
+    lane_to = lax.broadcasted_iota(jnp.int32, (middle, middle), 1)
+    free = span - span // 4
+    aside = ones((lane_to == lane_from + free) & ((lane_from & (span - 1)) < span // 4))
+
     def help_below():
         part = help_in.at[pl.ds(0, block * (half - 1))]
         pltpu.make_async_copy(part, part, help_sems.at[1]).wait()
@@ -442,7 +452,11 @@
         known = causal(
             products(help_in[:, state:], help_in[:middle, :state]), earlier[:, :middle]
         )
-        scores_out[...] = dot(fold, dot(known, swap).astype(bf16)).astype(bf16)
+        packed = dot(fold, dot(known, swap).astype(bf16))
+        moved = dot(packed[two : 2 * two].astype(bf16), aside)
+        scores_out[...] = jnp.concatenate(
+            [packed[2 * two : 3 * two], packed[3 * two : 4 * two] + moved, packed[4 * two :]]
+        ).astype(bf16)
         pltpu.make_async_remote_copy(
             src_ref=scores_out,
             dst_ref=scores_in,
@@ -463,7 +477,7 @@
 
             @pl.when(jnp.logical_not(tail))
             def _():
-                each(devices - 1, lambda step: send(sent.at[c], got.at[c], there_sems.at[c], far_peer(step)))
+                each(devices - 1, lambda step: send(sent.at[c], got.at[c], (x_sems.at[c], there_sems.at[c]), far_peer(step)))
 
         else:
 
@@ -471,7 +485,7 @@
             def _():
                 pl.semaphore_wait(late_sem, quarter)
                 each(quarter, lambda step: send_aux(late_peer(step)))
-                scatter_late(sent.at[c], got.at[c], there_sems.at[c])
+                scatter_late(sent.at[c], got.at[c], (x_sems.at[c], there_sems.at[c]))
 
         if c == 2:
 
@@ -539,10 +553,17 @@
             products(aux_in[middle:, state:], aux_in[middle:, :state]), earlier[middle:, middle:]
         )
         pltpu.make_async_copy(scores_in, scores_in, score_sems.at[1]).wait()
+        place = lax.broadcasted_iota(jnp.int32, (1, middle), 1)
+        came = scores_in[...].astype(f32)
+        shared = came[two : 2 * two]
+        moved = lax.dot_general(
+            shared.astype(bf16), aside, (((1,), (1,)), ((), ())), preferred_element_type=f32
+        )
+        stayed = jnp.where((place & (span - 1)) < free, shared, 0.0)
+        packed = jnp.concatenate([jnp.zeros_like(moved), moved, came[:two], stayed, came[2 * two :]])
         wide = lax.dot_general(
-            fold, scores_in[...], (((0,), (0,)), ((), ())), preferred_element_type=f32
-        )
-        place = lax.broadcasted_iota(jnp.int32, (1, middle), 1)
+            fold, packed.astype(bf16), (((0,), (0,)), ((), ())), preferred_element_type=f32
+        )
         wide = jnp.where(shift(place, middle // per) == (down & (per - 1)), wide, 0.0)
         col_scores[:, :middle] = lax.dot_general(
             wide.astype(bf16), swap, (((1,), (1,)), ((), ())), preferred_element_type=f32
@@ -564,11 +585,11 @@
         fade[c] = jnp.exp(-run)
 
     for c in range(chunks):
-        wait_either(got.at[c], there_sems.at[c, 1], tail)
+        wait_either(got.at[c], there_sems.at[c], tail)
         faded = (got[c].astype(f32) * fade[c]).astype(bf16)
         col_sent[c] = (grow[c] * dot(col_scores[...], faded)).astype(bf16)
-        give_back(col_sent.at[c], col_got.at[c], back_sems.at[c])
-        col_got[c, own, :] = col_sent[c, own, :]
+        give_back(col_sent.at[c], landing(c), (load_sems.at[c], back_sems.at[c]))
+        landing(c)[own, :] = col_sent[c, own, :]
 
     for c in range(chunks):
         cut = slice(c * width, (c + 1) * width)
@@ -613,7 +634,7 @@
     @pl.when(jnp.logical_not(tail))
     def _():
         for c in range(chunks):
-            wait(sent.at[c], there_sems.at[c, 0])
+            wait(sent.at[c], x_sems.at[c])
 
     total[...] = keep(total[...])
     rest_ref[...] = total[:, (chunks - 1) * width :]
@@ -622,22 +643,20 @@
         cut = slice(c * width, (c + 1) * width)
 
         if c:
-            wait_either(col_sent.at[c - 1], back_sems.at[c - 1, 0], head)
+            wait_either(col_sent.at[c - 1], load_sems.at[c - 1], head)
 
         @pl.when(head)
         def _():
-            col_got[c] = jnp.zeros((patches, width), bf16)
+            landing(c)[...] = jnp.zeros((patches, width), bf16)
 
         @pl.when(jnp.logical_not(head))
         def _():
-            wait(col_got.at[c], back_sems.at[c, 1])
-
-        if c == chunks - 1:
-            final_ref[...] = col_got[c]
-        else:
+            wait(landing(c), back_sems.at[c])
+
+        if c < chunks - 1:
             out_ref[:, cut] = (total[:, cut] + dot(restore, col_got[c])).astype(bf16)
 
-    wait_either(col_sent.at[chunks - 1], back_sems.at[chunks - 1, 0], head)
+    wait_either(col_sent.at[chunks - 1], load_sems.at[chunks - 1], head)
 
 
 def finish_kernel(done, rest, final, restore, out_hbm, last, sems):
@@ -674,7 +693,7 @@
     piece = (CHUNKS, patches, width)
     aux = pltpu.VMEM((patches, 2 * state), jnp.bfloat16)
     per = tile_cols // devices
-    scores = pltpu.VMEM((patches // per, patches // 2), jnp.bfloat16)
+    scores = pltpu.VMEM((patches // per * 3 // 4, patches // 2), jnp.bfloat16)
     decays = pltpu.VMEM((devices, tile_rows, per * heads), jnp.bfloat16)
     result = pl.pallas_call(
         functools.partial(fused_kernel, (devices, tile_rows, tile_cols, heads)),
@@ -720,8 +739,8 @@
             pltpu.SemaphoreType.DMA((2,)),
             pltpu.SemaphoreType.DMA((2,)),
             pltpu.SemaphoreType.DMA((3, 2)),
-            pltpu.SemaphoreType.DMA((CHUNKS, 2)),
-            pltpu.SemaphoreType.DMA((CHUNKS, 2)),
+            pltpu.SemaphoreType.DMA((CHUNKS,)),
+            pltpu.SemaphoreType.DMA((CHUNKS,)),
             pltpu.SemaphoreType.REGULAR,
         ],
         compiler_params=pltpu.CompilerParams(
@@ -756,7 +775,7 @@
         lax.axis_size("col") == 1
         and tile_mask.shape[1] == 1
         and tile_rows * devices == tile_cols
-        and devices % 4 == 0
+        and devices == 16
         and tile_cols <= 64
         and (tile_rows * (tile_cols // devices)) % 16 == 0
         and span_width % (CHUNKS * 128) == 0

time: 51.5 us -> 51.2 us (level)
  no operation moved by 1% of the time
where the time goes in v11:
time: 51.2 us; the launch traced here: 51.1 us
  Pallas kernels  51 us (100%)
    pallas_call x1, Pallas kernels, fused(): pl.pallas_call(functools.partial(fused_kernel, (devices, tile_rows, tile_...  50 us

profile of v11, /device:TPU:31, one launch (start us, length us, event | category | flops | bytes accessed | tf_op | source)
XLA Modules:
  0.0 51.1 jit_solution(7753829893834473947)
XLA Ops:
  0.0 50.0 %shard_map.73 = (bf16[256,1536]{1,0:T(8,128)(2,1)S(1)}, f32[256,512]{1,0:T(8,128)S(1)}, bf16[256,512]{1,0:T(8,128)(2,1)S(1)}, bf16[256,256]{1,0:T(8,128)(2,1)S(1)}) custom-call(s32[4]{0:T(128)} %bitcast.13, f32[1,32]{1,0:T(1,128)} %bitcast.14, bf16[256,2048]{1,0:T(8,128)(2,1)} %bitcast.8, bf16[256,128]{1,0:T(8,128)(2,1)} %bitcast.9, ...), custom_call_target="tpu_custom_call" | custom-call | tf_op jit(solution)/shard_map/pallas_call | solution.py:698
  50.1 1.0 %shard_map.74 = bf16[256,2048]{1,0:T(8,128)(2,1)} custom-call(bf16[256,1536]{1,0:T(8,128)(2,1)S(1)} %get-tuple-element.9.done, f32[256,512]{1,0:T(8,128)S(1)} %get-tuple-element.10.rest, bf16[256,512]{1,0:T(8,128)(2,1)S(1)} %get-tuple-element.11.final, bf16[256,256]{1,0:T(8,128)(2,1)S(1)} %get-tuple-element.12.restore), custom_call_target="tpu_custom_call" | custom-call | tf_op jit(solution)/shard_map/pallas_call | solution.py:758

commit v12 on v11

--- a/solution.py
+++ b/solution.py
@@ -205,8 +205,10 @@
         return jnp.where(upper, across_first, lax.rem(me + 1 + step, soon + 1))
 
     def far_peer(step):
+        place = lax.rem(me + step, half)
+        place = lax.shift_right_logical(place, 1) + (place & 1) * quarter
         across_first = jnp.where(
-            step < half, half + lax.rem(me + step, half), lax.rem(me + 1 + step - half, half)
+            step < half, half + place, lax.rem(me + 1 + step - half, half)
         )
         return jnp.where(upper, across_first, peer(step))
 
@@ -231,7 +233,14 @@
 
     @pl.when(jnp.logical_not(last))
     def _():
-        each(devices - 1, lambda step: greet(lax.rem(me - 1 - step + devices, devices)))
+        def act(step):
+            other = lax.rem(me - lax.rem(me, quarter) - 1 - step + devices, devices)
+
+            @pl.when(other != me)
+            def _():
+                greet(other)
+
+        each(devices, act)
 
     loads = [
         pltpu.make_async_copy(source, target, load_sems.at[i])
@@ -280,7 +289,7 @@
 
     def give_back(source, target, sems):
         def act(step):
-            other = peer(step)
+            other = far_peer(step)
 
             @pl.when(other >= 2)
             def _():
@@ -301,6 +310,7 @@
         def _():
             wait(buffer, sem, devices - 3)
 
+    pair_away = [load_sems.at[4], load_sems.at[5], pair_sems.at[3]]
     pairs = [(x_ref, pair_x), (kept_write, pair_write), (col_ref, pair_col)]
 
     def shift(i, size):
@@ -493,14 +503,17 @@
             def _():
                 help_below()
 
+    for load in loads[4:]:
+        load.wait()
+
     @pl.when(jnp.logical_not(odd))
     def _():
         for i, (source, target) in enumerate(pairs):
             pltpu.make_async_remote_copy(
                 src_ref=source,
                 dst_ref=target,
-                send_sem=pair_sems.at[i, 0],
-                recv_sem=pair_sems.at[i, 1],
+                send_sem=pair_away[i],
+                recv_sem=pair_sems.at[i],
                 device_id={"row": me + 1},
                 device_id_type=MESH,
             ).start()
@@ -517,8 +530,6 @@
     restore = keep((down == home(across)).astype(f32)).astype(bf16)
     in_row = (down >= across) & (shift(down, tile_cols) == shift(across, tile_cols))
     row_below = ones(in_row)
-    for load in loads[4:]:
-        load.wait()
     row_decays = turned(down, row_ref)
     own_scores = products(read_ref[...], write_ref[...])
     row_scores = causal(own_scores, in_row)
@@ -601,7 +612,7 @@
     @pl.when(odd)
     def _():
         for i, (source, target) in enumerate(pairs):
-            pltpu.make_async_copy(target, target, pair_sems.at[i, 1]).wait()
+            pltpu.make_async_copy(target, target, pair_sems.at[i]).wait()
         alike = (down & (tile_cols - 1)) == (across & (tile_cols - 1))
         pair_after = ones((shift(down, tile_cols) < shift(across, tile_cols)) & alike)
         pair_decays = turned(down, pair_col)
@@ -615,7 +626,7 @@
     @pl.when(jnp.logical_not(odd))
     def _():
         for i, (source, target) in enumerate(pairs):
-            pltpu.make_async_copy(source, source, pair_sems.at[i, 0]).wait()
+            pltpu.make_async_copy(source, source, pair_away[i]).wait()
 
     pltpu.make_async_copy(pieces, pieces, decay_sems.at[0]).wait()
 
@@ -738,7 +749,7 @@
             pltpu.SemaphoreType.DMA((3,)),
             pltpu.SemaphoreType.DMA((2,)),
             pltpu.SemaphoreType.DMA((2,)),
-            pltpu.SemaphoreType.DMA((3, 2)),
+            pltpu.SemaphoreType.DMA((4,)),
             pltpu.SemaphoreType.DMA((CHUNKS,)),
             pltpu.SemaphoreType.DMA((CHUNKS,)),
             pltpu.SemaphoreType.REGULAR,

time: 51.2 us -> 51 us (level)
  the two profiles are of different devices: /device:TPU:31 before, /device:TPU:25 now
where the time goes in v12:
time: 51 us; the launch traced here: 50.9 us
  Pallas kernels  50.9 us (100%)
    pallas_call x1, Pallas kernels, fused(): pl.pallas_call(functools.partial(fused_kernel, (devices, tile_rows, tile_...  49.9 us

profile of v12, /device:TPU:25, one launch (start us, length us, event | category | flops | bytes accessed | tf_op | source)
XLA Modules:
  0.0 50.9 jit_solution(1371763070688506575)
XLA Ops:
  0.0 49.9 %shard_map.73 = (bf16[256,1536]{1,0:T(8,128)(2,1)S(1)}, f32[256,512]{1,0:T(8,128)S(1)}, bf16[256,512]{1,0:T(8,128)(2,1)S(1)}, bf16[256,256]{1,0:T(8,128)(2,1)S(1)}) custom-call(s32[4]{0:T(128)} %bitcast.13, f32[1,32]{1,0:T(1,128)} %bitcast.14, bf16[256,2048]{1,0:T(8,128)(2,1)} %bitcast.8, bf16[256,128]{1,0:T(8,128)(2,1)} %bitcast.9, ...), custom_call_target="tpu_custom_call" | custom-call | tf_op jit(solution)/shard_map/pallas_call | solution.py:709
  49.9 1.0 %shard_map.74 = bf16[256,2048]{1,0:T(8,128)(2,1)} custom-call(bf16[256,1536]{1,0:T(8,128)(2,1)S(1)} %get-tuple-element.9.done, f32[256,512]{1,0:T(8,128)S(1)} %get-tuple-element.10.rest, bf16[256,512]{1,0:T(8,128)(2,1)S(1)} %get-tuple-element.11.final, bf16[256,256]{1,0:T(8,128)(2,1)S(1)} %get-tuple-element.12.restore), custom_call_target="tpu_custom_call" | custom-call | tf_op jit(solution)/shard_map/pallas_call | solution.py:769
